TPU v7x, 128 devices: a whole 4x4x4 slice. The times are simulated.
128 devices in a mesh: tile: 64 (over z, x, y), view: 2 (over core).
Axes of the slice: x: 4, y: 4, z: 4, core: 2. Of those that a mesh axis runs over, the one named last changes fastest.
Arguments:
- estimate: float32 [1024, 128, 128], P('tile'), may hold values from 0.5 to 2
- view_data: float32 [6, 1024, 128, 128], P('view', 'tile'), may hold values from 0.2 to 5
- psf_taps: float32 [6, 3, 31], P('view'), may hold values from 0.05 to 1
- coverage: int32 [6, 1024], P('view', 'tile'), may hold values 0 or 1
Outputs:
- deconvolved: float32 [1024, 128, 128], P('tile')
All inputs are finite; a program needn't handle non-finite values. No bound on the sum of `coverage` on one device may be relied on, other than what follows from the above.
Results may differ from a plain program's by a relative error of at most 0.00012.
Values sent between devices are 32-bit elements; how exact they have to be, the bound alone decides.
No kernel may reach another device: no remote copies, remote signals or barrier semaphores. Data moves between devices by JAX's collectives and lax.ppermute only.
A program may use at most 128 MiB of HBM per device.

v0:
```python
import jax
import jax.numpy as jnp
from jax import lax
from jax.sharding import PartitionSpec as P

ITERS = 4


def with_halo(block, sides, width):
    for axis, dim in sides:
        count = lax.axis_size(axis)
        forward = [(i, i + 1) for i in range(count - 1)]
        backward = [(target, source) for source, target in forward]
        low = lax.ppermute(
            lax.slice_in_dim(block, block.shape[dim] - width, None, axis=dim), axis, forward
        )
        high = lax.ppermute(lax.slice_in_dim(block, 0, width, axis=dim), axis, backward)
        block = jnp.concatenate([low, block, high], axis=dim)
    return block


def shifted(x, axis, by):
    size = lax.axis_size(axis)
    pairs = [(i, i + by) for i in range(size) if 0 <= i + by < size]
    return lax.ppermute(x, axis, pairs)


def make_band(taps, rows, columns, offset):
    row_index = jnp.arange(rows)[:, None]
    column_index = jnp.arange(columns)[None, :]
    spacing = column_index - row_index + offset
    matrix = jnp.zeros((rows, columns), jnp.float32)
    for lag in range(taps.shape[0]):
        matrix = matrix + taps[lag] * (spacing == lag).astype(jnp.float32)
    return matrix


def stack_bands(taps_rows, rows, columns, offset):
    return jnp.stack(
        [make_band(taps_rows[which], rows, columns, offset) for which in range(taps_rows.shape[0])]
    )


def blur_inner(volume, y_stack, z_stack):
    hp = lax.Precision.HIGHEST
    volume = jnp.einsum("vxyz,vwy->vxwz", volume, y_stack, precision=hp)
    return jnp.einsum("vxyz,vwz->vxyw", volume, z_stack, precision=hp)


def adjoint_inner(volume, y_stack, z_stack):
    hp = lax.Precision.HIGHEST
    volume = jnp.einsum("vxyz,vzw->vxyw", volume, z_stack, precision=hp)
    return jnp.einsum("vxyz,vyw->vxwz", volume, y_stack, precision=hp)


def per_device(estimate, view_data, psf_taps, coverage):
    hp = lax.Precision.HIGHEST
    norm_taps = psf_taps / jnp.sum(psf_taps, axis=-1, keepdims=True)
    reach = norm_taps.shape[-1] // 2
    width, depth_y, depth_z = estimate.shape
    weights = coverage.astype(jnp.float32)
    count = lax.psum(jnp.sum(weights, axis=0), "view")
    keep = 1.0 - jnp.minimum(count, 1.0)
    denom = jnp.maximum(count, 1.0)
    y_stack = stack_bands(norm_taps[:, 1], depth_y, depth_y, reach)
    z_stack = stack_bands(norm_taps[:, 2], depth_z, depth_z, reach)
    x_forward = stack_bands(norm_taps[:, 0], width, width + 2 * reach, 0)
    x_spread = stack_bands(norm_taps[:, 0][:, ::-1], width + 2 * reach, width, 2 * reach)
    cover_wide = with_halo(coverage, (("tile", 1),), reach).astype(jnp.float32)
    current = estimate
    for iteration in range(ITERS):
        padded = with_halo(current, (("tile", 0),), reach)
        first = jnp.einsum("xyz,vwx->vwyz", padded, x_forward, precision=hp)
        blurred = blur_inner(first, y_stack, z_stack)
        inner = adjoint_inner(view_data / blurred, y_stack, z_stack)
        spread = jnp.einsum("vxyz,vwx->vwyz", inner, x_spread, precision=hp)
        wide_total = jnp.einsum("vx,vxyz->xyz", cover_wide, spread, precision=hp)
        from_below = shifted(wide_total[width + reach :], "tile", 1)
        from_above = shifted(wide_total[:reach], "tile", -1)
        total = wide_total[reach : reach + width]
        total = total.at[:reach].add(from_below)
        total = total.at[width - reach :].add(from_above)
        summed = lax.psum(total, "view")
        current = current * (summed + keep[:, None, None]) / denom[:, None, None]
    return current


def solution(mesh):
    return jax.shard_map(
        per_device,
        mesh=mesh,
        in_specs=(
            P("tile", None, None),
            P("view", "tile", None, None),
            P("view", None, None),
            P("view", "tile"),
        ),
        out_specs=P("tile", None, None),
        check_vma=False,
    )
```

profile of v0, /device:TPU:1, one launch (start us, length us, event | category | flops | bytes accessed | tf_op | source)
XLA Modules:
  0.0 885.3 jit_solution(16694001589584169548)
XLA Ops:
  7.4 4.0 collective-permute-start
  15.9 4.0 collective-permute-start.2
  36.5 19.5 %select_add_fusion.10 = f32[1,46,16]{1,2,0:T(8,128)S(1)} fusion(f32[]{:T(128)} %bitcast.64, f32[]{:T(128)} %bitcast.63, f32[]{:T(128)} %bitcast.62, f32[]{:T(128)} %bitcast.61, f32[]{:T(128)} %bitcast.60, f32[]{:T(128)} %bitcast.59, f32[]{:T(128)} %bitcast.58, f32[]{:T(128)} %bitcast.57, f32[]{:T(128)} %bitcast.56, f32[]{:T(128)} %bitcast.55, f32[]{:T(128)} %bitcast.54, ...), kind=kLoop, calls=%fused_computation.154 | loop fusion | flops 69184 | bytes 3068 | tf_op jit(solution)/shard_map/add | solution.py:34
  56.0 19.3 %select_add_fusion.9 = f32[1,46,16]{1,2,0:T(8,128)S(1)} fusion(f32[]{:T(128)} %bitcast.96, f32[]{:T(128)} %bitcast.95, f32[]{:T(128)} %bitcast.94, f32[]{:T(128)} %bitcast.93, f32[]{:T(128)} %bitcast.92, f32[]{:T(128)} %bitcast.91, f32[]{:T(128)} %bitcast.90, f32[]{:T(128)} %bitcast.89, f32[]{:T(128)} %bitcast.88, f32[]{:T(128)} %bitcast.87, f32[]{:T(128)} %bitcast.86, ...), kind=kLoop, calls=%fused_computation.153 | loop fusion | flops 69184 | bytes 3068 | tf_op jit(solution)/shard_map/add | solution.py:34
  75.3 19.2 %select_add_fusion.11 = f32[1,46,16]{1,2,0:T(8,128)S(1)} fusion(f32[]{:T(128)} %bitcast.32, f32[]{:T(128)} %bitcast.31, f32[]{:T(128)} %bitcast.30, f32[]{:T(128)} %bitcast.29, f32[]{:T(128)} %bitcast.28, f32[]{:T(128)} %bitcast.27, f32[]{:T(128)} %bitcast.26, f32[]{:T(128)} %bitcast.25, f32[]{:T(128)} %bitcast.24, f32[]{:T(128)} %bitcast.23, f32[]{:T(128)} %bitcast.22, ...), kind=kLoop, calls=%fused_computation.155 | loop fusion | flops 69184 | bytes 3068 | tf_op jit(solution)/shard_map/add | solution.py:34
  94.5 19.4 %select_add_fusion.6 = f32[1,16,46]{2,1,0:T(8,128)S(1)} fusion(f32[]{:T(128)} %bitcast.287, f32[]{:T(128)} %bitcast.286, f32[]{:T(128)} %bitcast.285, f32[]{:T(128)} %bitcast.284, f32[]{:T(128)} %bitcast.283, f32[]{:T(128)} %bitcast.282, f32[]{:T(128)} %bitcast.281, f32[]{:T(128)} %bitcast.280, f32[]{:T(128)} %bitcast.279, f32[]{:T(128)} %bitcast.278, ...), kind=kLoop, calls=%fused_computation.118 | loop fusion | flops 68448 | bytes 3068 | tf_op jit(solution)/shard_map/add | solution.py:34
  114.0 19.5 %select_add_fusion.7 = f32[1,16,46]{2,1,0:T(8,128)S(1)} fusion(f32[]{:T(128)} %bitcast.256, f32[]{:T(128)} %bitcast.255, f32[]{:T(128)} %bitcast.254, f32[]{:T(128)} %bitcast.253, f32[]{:T(128)} %bitcast.252, f32[]{:T(128)} %bitcast.251, f32[]{:T(128)} %bitcast.250, f32[]{:T(128)} %bitcast.249, f32[]{:T(128)} %bitcast.248, f32[]{:T(128)} %bitcast.247, ...), kind=kLoop, calls=%fused_computation.119 | loop fusion | flops 68448 | bytes 3068 | tf_op jit(solution)/shard_map/add | solution.py:34
  133.5 19.5 %select_add_fusion = f32[1,128,128]{2,1,0:T(8,128)S(1)} fusion(f32[]{:T(128)} %bitcast.385, f32[]{:T(128)} %bitcast.384, f32[]{:T(128)} %bitcast.383, f32[]{:T(128)} %bitcast.382, f32[]{:T(128)} %bitcast.381, f32[]{:T(128)} %bitcast.380, f32[]{:T(128)} %bitcast.379, f32[]{:T(128)} %bitcast.378, f32[]{:T(128)} %bitcast.377, f32[]{:T(128)} %bitcast.376, ...), kind=kLoop, calls=%fused_computation.78 | loop fusion | flops 1540096 | bytes 65660 | tf_op jit(solution)/shard_map/add | solution.py:34
  153.1 19.8 %select_add_fusion.5 = f32[1,128,128]{2,1,0:T(8,128)S(1)} fusion(f32[]{:T(128)} %bitcast.129, f32[]{:T(128)} %bitcast.128, f32[]{:T(128)} %bitcast.127, f32[]{:T(128)} %bitcast.126, f32[]{:T(128)} %bitcast.125, f32[]{:T(128)} %bitcast.124, f32[]{:T(128)} %bitcast.123, f32[]{:T(128)} %bitcast.122, f32[]{:T(128)} %bitcast.121, f32[]{:T(128)} %bitcast.120, ...), kind=kLoop, calls=%fused_computation.83 | loop fusion | flops 1540096 | bytes 65660 | tf_op jit(solution)/shard_map/add | solution.py:34
  172.9 19.1 %select_add_fusion.2 = f32[1,128,128]{2,1,0:T(8,128)S(1)} fusion(f32[]{:T(128)} %bitcast.323, f32[]{:T(128)} %bitcast.322, f32[]{:T(128)} %bitcast.321, f32[]{:T(128)} %bitcast.320, f32[]{:T(128)} %bitcast.319, f32[]{:T(128)} %bitcast.318, f32[]{:T(128)} %bitcast.317, f32[]{:T(128)} %bitcast.316, f32[]{:T(128)} %bitcast.315, f32[]{:T(128)} %bitcast.314, ...), kind=kLoop, calls=%fused_computation.80 | loop fusion | flops 1540096 | bytes 65660 | tf_op jit(solution)/shard_map/add | solution.py:34
  192.0 19.7 %select_add_fusion.3 = f32[1,128,128]{2,1,0:T(8,128)S(1)} fusion(f32[]{:T(128)} %bitcast.191, f32[]{:T(128)} %bitcast.190, f32[]{:T(128)} %bitcast.189, f32[]{:T(128)} %bitcast.188, f32[]{:T(128)} %bitcast.187, f32[]{:T(128)} %bitcast.186, f32[]{:T(128)} %bitcast.185, f32[]{:T(128)} %bitcast.184, f32[]{:T(128)} %bitcast.183, f32[]{:T(128)} %bitcast.182, ...), kind=kLoop, calls=%fused_computation.81 | loop fusion | flops 1540096 | bytes 65660 | tf_op jit(solution)/shard_map/add | solution.py:34
  211.7 19.4 %select_add_fusion.4 = f32[1,128,128]{2,1,0:T(8,128)S(1)} fusion(f32[]{:T(128)} %bitcast.160, f32[]{:T(128)} %bitcast.159, f32[]{:T(128)} %bitcast.158, f32[]{:T(128)} %bitcast.157, f32[]{:T(128)} %bitcast.156, f32[]{:T(128)} %bitcast.155, f32[]{:T(128)} %bitcast.154, f32[]{:T(128)} %bitcast.153, f32[]{:T(128)} %bitcast.152, f32[]{:T(128)} %bitcast.151, ...), kind=kLoop, calls=%fused_computation.82 | loop fusion | flops 1540096 | bytes 65660 | tf_op jit(solution)/shard_map/add | solution.py:34
  231.1 19.6 %select_add_fusion.1 = f32[1,128,128]{2,1,0:T(8,128)S(1)} fusion(f32[]{:T(128)} %bitcast.354, f32[]{:T(128)} %bitcast.353, f32[]{:T(128)} %bitcast.352, f32[]{:T(128)} %bitcast.351, f32[]{:T(128)} %bitcast.350, f32[]{:T(128)} %bitcast.349, f32[]{:T(128)} %bitcast.348, f32[]{:T(128)} %bitcast.347, f32[]{:T(128)} %bitcast.346, f32[]{:T(128)} %bitcast.345, ...), kind=kLoop, calls=%fused_computation.79 | loop fusion | flops 1540096 | bytes 65660 | tf_op jit(solution)/shard_map/add | solution.py:34
  250.7 19.1 %select_add_fusion.8 = f32[1,16,46]{2,1,0:T(8,128)S(1)} fusion(f32[]{:T(128)} %bitcast.225, f32[]{:T(128)} %bitcast.224, f32[]{:T(128)} %bitcast.223, f32[]{:T(128)} %bitcast.222, f32[]{:T(128)} %bitcast.221, f32[]{:T(128)} %bitcast.220, f32[]{:T(128)} %bitcast.219, f32[]{:T(128)} %bitcast.218, f32[]{:T(128)} %bitcast.217, f32[]{:T(128)} %bitcast.216, ...), kind=kLoop, calls=%fused_computation.120 | loop fusion | flops 68448 | bytes 3068 | tf_op jit(solution)/shard_map/add | solution.py:34
  270.3 4.6 fusion.42
  274.9 4.0 fusion.40
  288.0 20.5 %fusion.20 = f32[3,46,128,128]{3,1,2,0:T(8,128)S(1)} fusion(f32[3,128,16,128]{3,1,2,0:T(8,128)S(1)} %fusion.165, f32[1,46,16]{1,2,0:T(8,128)S(1)} %select_add_fusion.9, f32[1,46,16]{1,2,0:T(8,128)S(1)} %select_add_fusion.10, f32[1,46,16]{1,2,0:T(8,128)S(1)} %select_add_fusion.11), kind=kOutput, calls=%fused_computation.20 | convolution fusion | flops 434114880 | bytes 12198528 | tf_op jit(solution)/shard_map/vxyz,vwx->vwyz/dot_general | solution.py:76
  308.5 34.5 %fusion.6 = f32[46,1,128,128]{3,1,2,0:T(1,128)S(1)} fusion(f32[3,46,1,1]{0,2,3,1:T(1,128)S(1)} %copy.15, f32[3,46,128,128]{3,1,2,0:T(8,128)S(1)} %fusion.20), kind=kOutput, calls=%fused_computation.6 | convolution fusion | flops 27131904 | bytes 12059176 | tf_op jit(solution)/shard_map/vx,vxyz->xyz/dot_general | solution.py:77
  343.1 4.1 collective-permute-start.4
  348.6 17.8 %collective-permute-done.4 = f32[15,128,128]{2,1,0:T(8,128)S(1)} collective-permute-done((f32[15,128,128]{2,1,0:T(8,128)S(1)}, f32[15,128,128]{2,1,0:T(8,128)S(1)}, u32[]{:S(2)}, u32[]{:S(2)}) %collective-permute-start.4) | collective-permute-done | bytes 983072 | tf_op jit(solution)/shard_map/ppermute | solution.py:25
  366.5 3.8 collective-permute-done.5
  371.6 5.1 psum.36
  376.7 36.8 %all-reduce.5.cloned.1.call-done = f32[16,128,128]{2,1,0:T(8,128)} async-done(((f32[16,128,128]{2,1,0:T(8,128)}), f32[16,128,128]{2,1,0:T(8,128)}) %all-reduce.5.cloned.1.call-update) | async-done | bytes 1048592 | tf_op jit(solution)/shard_map/psum | solution.py:83
  420.2 19.1 %collective-permute-done.6 = f32[15,128,128]{2,1,0:T(8,128)S(1)} collective-permute-done((f32[15,128,128]{2,1,0:T(8,128)S(1)}, f32[15,128,128]{2,1,0:T(8,128)S(1)}, u32[]{:S(2)}, u32[]{:S(2)}) %collective-permute-start.6) | collective-permute-done | bytes 983072 | tf_op jit(solution)/shard_map/ppermute | solution.py:14
  439.4 3.9 collective-permute-done.7
  443.5 4.6 fusion.37
  448.1 3.7 fusion.35
  461.1 8.9 %fusion.16 = f32[3,46,128,128]{3,1,2,0:T(8,128)S(1)} fusion(f32[3,128,16,128]{3,1,2,0:T(8,128)S(1)} %fusion.164, f32[1,46,16]{1,2,0:T(8,128)S(1)} %select_add_fusion.9, f32[1,46,16]{1,2,0:T(8,128)S(1)} %select_add_fusion.10, f32[1,46,16]{1,2,0:T(8,128)S(1)} %select_add_fusion.11), kind=kOutput, calls=%fused_computation.16 | convolution fusion | flops 434114880 | bytes 12198528 | tf_op jit(solution)/shard_map/vxyz,vwx->vwyz/dot_general | solution.py:76
  470.0 34.5 %fusion.4 = f32[46,1,128,128]{3,1,2,0:T(1,128)S(1)} fusion(f32[3,46,1,1]{0,2,3,1:T(1,128)S(1)} %copy.15, f32[3,46,128,128]{3,1,2,0:T(8,128)S(1)} %fusion.16), kind=kOutput, calls=%fused_computation.4 | convolution fusion | flops 27131904 | bytes 12059176 | tf_op jit(solution)/shard_map/vx,vxyz->xyz/dot_general | solution.py:77
  509.2 18.2 %collective-permute-done.8 = f32[15,128,128]{2,1,0:T(8,128)S(1)} collective-permute-done((f32[15,128,128]{2,1,0:T(8,128)S(1)}, f32[15,128,128]{2,1,0:T(8,128)S(1)}, u32[]{:S(2)}, u32[]{:S(2)}) %collective-permute-start.8) | collective-permute-done | bytes 983072 | tf_op jit(solution)/shard_map/ppermute | solution.py:25
  527.5 3.8 collective-permute-done.9
  532.6 35.2 %all-reduce.7.cloned.1.call-done = f32[16,128,128]{2,1,0:T(8,128)} async-done(((f32[16,128,128]{2,1,0:T(8,128)}), f32[16,128,128]{2,1,0:T(8,128)}) %all-reduce.7.cloned.1.call-update) | async-done | bytes 1048592 | tf_op jit(solution)/shard_map/psum | solution.py:83
  574.2 19.4 %collective-permute-done.10 = f32[15,128,128]{2,1,0:T(8,128)S(1)} collective-permute-done((f32[15,128,128]{2,1,0:T(8,128)S(1)}, f32[15,128,128]{2,1,0:T(8,128)S(1)}, u32[]{:S(2)}, u32[]{:S(2)}) %collective-permute-start.10) | collective-permute-done | bytes 983072 | tf_op jit(solution)/shard_map/ppermute | solution.py:14
  593.5 3.9 collective-permute-done.11
  597.7 4.6 fusion.32
  615.6 8.6 fusion.12
  624.2 34.5 %fusion.2 = f32[46,1,128,128]{3,1,2,0:T(1,128)S(1)} fusion(f32[3,46,1,1]{0,2,3,1:T(1,128)S(1)} %copy.15, f32[3,46,128,128]{3,1,2,0:T(8,128)S(1)} %fusion.12), kind=kOutput, calls=%fused_computation.2 | convolution fusion | flops 27131904 | bytes 12059176 | tf_op jit(solution)/shard_map/vx,vxyz->xyz/dot_general | solution.py:77
  663.4 18.2 %collective-permute-done.12 = f32[15,128,128]{2,1,0:T(8,128)S(1)} collective-permute-done((f32[15,128,128]{2,1,0:T(8,128)S(1)}, f32[15,128,128]{2,1,0:T(8,128)S(1)}, u32[]{:S(2)}, u32[]{:S(2)}) %collective-permute-start.12) | collective-permute-done | bytes 983072 | tf_op jit(solution)/shard_map/ppermute | solution.py:25
  681.7 3.8 collective-permute-done.13
  686.8 35.2 %all-reduce.9.cloned.1.call-done = f32[16,128,128]{2,1,0:T(8,128)} async-done(((f32[16,128,128]{2,1,0:T(8,128)}), f32[16,128,128]{2,1,0:T(8,128)}) %all-reduce.9.cloned.1.call-update) | async-done | bytes 1048592 | tf_op jit(solution)/shard_map/psum | solution.py:83
  728.6 19.1 %collective-permute-done.14 = f32[15,128,128]{2,1,0:T(8,128)S(1)} collective-permute-done((f32[15,128,128]{2,1,0:T(8,128)S(1)}, f32[15,128,128]{2,1,0:T(8,128)S(1)}, u32[]{:S(2)}, u32[]{:S(2)}) %collective-permute-start.14) | collective-permute-done | bytes 983072 | tf_op jit(solution)/shard_map/ppermute | solution.py:14
  747.8 3.9 collective-permute-done.15
  751.9 4.6 fusion.27
  769.6 8.7 fusion.8
  778.2 34.5 %fusion = f32[46,1,128,128]{3,1,2,0:T(1,128)S(1)} fusion(f32[3,46,1,1]{0,2,3,1:T(1,128)S(1)} %copy.15, f32[3,46,128,128]{3,1,2,0:T(8,128)S(1)} %fusion.8), kind=kOutput, calls=%fused_computation | convolution fusion | flops 27131904 | bytes 12059176 | tf_op jit(solution)/shard_map/vx,vxyz->xyz/dot_general | solution.py:77
  817.4 18.2 %collective-permute-done.16 = f32[15,128,128]{2,1,0:T(8,128)S(1)} collective-permute-done((f32[15,128,128]{2,1,0:T(8,128)S(1)}, f32[15,128,128]{2,1,0:T(8,128)S(1)}, u32[]{:S(2)}, u32[]{:S(2)}) %collective-permute-start.16) | collective-permute-done | bytes 983072 | tf_op jit(solution)/shard_map/ppermute | solution.py:25
  835.8 3.8 collective-permute-done.17
  840.8 35.2 %all-reduce.11.cloned.1.call-done = f32[16,128,128]{2,1,0:T(8,128)} async-done(((f32[16,128,128]{2,1,0:T(8,128)}), f32[16,128,128]{2,1,0:T(8,128)}) %all-reduce.11.cloned.1.call-update) | async-done | bytes 1048592 | tf_op jit(solution)/shard_map/psum | solution.py:83
  (120 shorter events, 110.4 us)
Async XLA Ops:
  6.5 14.7 %copy-start.6 = (f32[3,3,31]{2,1,0:T(4,128)S(1)}, f32[3,3,31]{2,1,0:T(4,128)}, u32[]{:S(2)}) copy-start(f32[3,3,31]{2,1,0:T(4,128)} %param.22) | copy-start | bytes 3352
  6.5 407.0 %all-reduce.5.cloned.1.call-start = ((), (), s32[]{:S(2)}) async-start(), calls=%async_computation | async-start | bytes 2097152 | tf_op jit(solution)/shard_map/psum | solution.py:83
  7.4 262.4 %collective-permute-start = (s32[3,15]{1,0:T(4,128)S(1)}, s32[3,15]{1,0:T(4,128)S(1)}, u32[]{:S(2)}, u32[]{:S(2)}) collective-permute-start(s32[3,15]{1,0:T(4,128)S(1)} %get-tuple-element.399), channel_id=1, source_target_pairs={{0,2},{2,4},{4,6},{6,8},{8,10},{10,12},{12,14},{14,16},{16,18},{18... | collective-permute-start | bytes 548 | tf_op jit(solution)/shard_map/ppermute | solution.py:14
  11.4 258.4 %copy-start.5 = (s32[3,16]{1,0:T(4,128)S(1)}, s32[3,16]{1,0:T(4,128)}, u32[]{:S(2)}) copy-start(s32[3,16]{1,0:T(4,128)} %param.23) | copy-start | bytes 580
  11.4 258.6 %copy-start = (f32[16,128,128]{2,1,0:T(8,128)S(1)}, f32[16,128,128]{2,1,0:T(8,128)}, u32[]{:S(2)}) copy-start(f32[16,128,128]{2,1,0:T(8,128)} %param.20) | copy-start | bytes 3145732
  11.4 258.4 %collective-permute-start.1 = (s32[3,15]{1,0:T(4,128)S(1)}, s32[3,15]{1,0:T(4,128)S(1)}, u32[]{:S(2)}, u32[]{:S(2)}) collective-permute-start(s32[3,15]{1,0:T(4,128)S(1)} %get-tuple-element.400), channel_id=1, source_target_pairs={{2,0},{4,2},{6,4},{8,6},{10,8},{12,10},{14,12},{16,14},{18,16},{20... | collective-permute-start | bytes 548 | tf_op jit(solution)/shard_map/ppermute | solution.py:17
  15.9 254.2 %collective-permute-start.2 = (f32[15,128,128]{2,1,0:T(8,128)}, f32[15,128,128]{2,1,0:T(8,128)S(1)}, u32[]{:S(2)}, u32[]{:S(2)}) collective-permute-start(f32[15,128,128]{2,1,0:T(8,128)} %get-tuple-element.115), channel_id=1, source_target_pairs={{0,2},{2,4},{4,6},{6,8},{8,10},{10,12},{12,14},{14,16},{16,18},{18... | collective-permute-start | bytes 2949128 | tf_op jit(solution)/shard_map/ppermute | solution.py:14
  19.9 250.1 %collective-permute-start.3 = (f32[15,128,128]{2,1,0:T(8,128)}, f32[15,128,128]{2,1,0:T(8,128)S(1)}, u32[]{:S(2)}, u32[]{:S(2)}) collective-permute-start(f32[15,128,128]{2,1,0:T(8,128)} %get-tuple-element.116), channel_id=1, source_target_pairs={{2,0},{4,2},{6,4},{8,6},{10,8},{12,10},{14,12},{16,14},{18,16},{20... | collective-permute-start | bytes 2949128 | tf_op jit(solution)/shard_map/ppermute | solution.py:17
  278.9 2.9 copy-start.7
  343.1 23.2 %collective-permute-start.4 = (f32[15,128,128]{2,1,0:T(8,128)S(1)}, f32[15,128,128]{2,1,0:T(8,128)S(1)}, u32[]{:S(2)}, u32[]{:S(2)}) collective-permute-start(f32[15,128,128]{2,1,0:T(8,128)S(1)} %get-tuple-element.108), channel_id=1, source_target_pairs={{0,2},{2,4},{4,6},{6,8},{8,10},{10,12},{12,14},{14,16},{16,18},{18... | collective-permute-start | bytes 2949128 | tf_op jit(solution)/shard_map/ppermute | solution.py:25
  347.2 23.1 %collective-permute-start.5 = (f32[15,128,128]{2,1,0:T(8,128)S(1)}, f32[15,128,128]{2,1,0:T(8,128)S(1)}, u32[]{:S(2)}, u32[]{:S(2)}) collective-permute-start(f32[15,128,128]{2,1,0:T(8,128)S(1)} %get-tuple-element.107), channel_id=1, source_target_pairs={{2,0},{4,2},{6,4},{8,6},{10,8},{12,10},{14,12},{16,14},{18,16},{20... | collective-permute-start | bytes 2949128 | tf_op jit(solution)/shard_map/ppermute | solution.py:25
  370.5 1.0 copy-start.1
  371.5 196.2 %all-reduce.7.cloned.1.call-start = ((), (), s32[]{:S(2)}) async-start(), calls=%async_computation.1 | async-start | bytes 2097152 | tf_op jit(solution)/shard_map/psum | solution.py:83
  415.2 24.1 %collective-permute-start.6 = (f32[15,128,128]{2,1,0:T(8,128)S(1)}, f32[15,128,128]{2,1,0:T(8,128)S(1)}, u32[]{:S(2)}, u32[]{:S(2)}) collective-permute-start(f32[15,128,128]{2,1,0:T(8,128)S(1)} %get-tuple-element.113), channel_id=1, source_target_pairs={{0,2},{2,4},{4,6},{6,8},{8,10},{10,12},{12,14},{14,16},{16,18},{18... | collective-permute-start | bytes 2949128 | tf_op jit(solution)/shard_map/ppermute | solution.py:14
  418.5 24.7 %collective-permute-start.7 = (f32[15,128,128]{2,1,0:T(8,128)S(1)}, f32[15,128,128]{2,1,0:T(8,128)S(1)}, u32[]{:S(2)}, u32[]{:S(2)}) collective-permute-start(f32[15,128,128]{2,1,0:T(8,128)S(1)} %get-tuple-element.114), channel_id=1, source_target_pairs={{2,0},{4,2},{6,4},{8,6},{10,8},{12,10},{14,12},{16,14},{18,16},{20... | collective-permute-start | bytes 2949128 | tf_op jit(solution)/shard_map/ppermute | solution.py:17
  451.9 2.9 copy-start.8
  504.7 22.7 %collective-permute-start.8 = (f32[15,128,128]{2,1,0:T(8,128)S(1)}, f32[15,128,128]{2,1,0:T(8,128)S(1)}, u32[]{:S(2)}, u32[]{:S(2)}) collective-permute-start(f32[15,128,128]{2,1,0:T(8,128)S(1)} %get-tuple-element.106), channel_id=1, source_target_pairs={{0,2},{2,4},{4,6},{6,8},{8,10},{10,12},{12,14},{14,16},{16,18},{18... | collective-permute-start | bytes 2949128 | tf_op jit(solution)/shard_map/ppermute | solution.py:25
  507.8 23.5 %collective-permute-start.9 = (f32[15,128,128]{2,1,0:T(8,128)S(1)}, f32[15,128,128]{2,1,0:T(8,128)S(1)}, u32[]{:S(2)}, u32[]{:S(2)}) collective-permute-start(f32[15,128,128]{2,1,0:T(8,128)S(1)} %get-tuple-element.105), channel_id=1, source_target_pairs={{2,0},{4,2},{6,4},{8,6},{10,8},{12,10},{14,12},{16,14},{18,16},{20... | collective-permute-start | bytes 2949128 | tf_op jit(solution)/shard_map/ppermute | solution.py:25
  531.5 1.0 copy-start.2
  532.5 189.5 %all-reduce.9.cloned.1.call-start = ((), (), s32[]{:S(2)}) async-start(), calls=%async_computation.2 | async-start | bytes 2097152 | tf_op jit(solution)/shard_map/psum | solution.py:83
  569.4 24.1 %collective-permute-start.10 = (f32[15,128,128]{2,1,0:T(8,128)S(1)}, f32[15,128,128]{2,1,0:T(8,128)S(1)}, u32[]{:S(2)}, u32[]{:S(2)}) collective-permute-start(f32[15,128,128]{2,1,0:T(8,128)S(1)} %get-tuple-element.111), channel_id=1, source_target_pairs={{0,2},{2,4},{4,6},{6,8},{8,10},{10,12},{12,14},{14,16},{16,18},{18... | collective-permute-start | bytes 2949128 | tf_op jit(solution)/shard_map/ppermute | solution.py:14
  572.7 24.7 %collective-permute-start.11 = (f32[15,128,128]{2,1,0:T(8,128)S(1)}, f32[15,128,128]{2,1,0:T(8,128)S(1)}, u32[]{:S(2)}, u32[]{:S(2)}) collective-permute-start(f32[15,128,128]{2,1,0:T(8,128)S(1)} %get-tuple-element.112), channel_id=1, source_target_pairs={{2,0},{4,2},{6,4},{8,6},{10,8},{12,10},{14,12},{16,14},{18,16},{20... | collective-permute-start | bytes 2949128 | tf_op jit(solution)/shard_map/ppermute | solution.py:17
  606.1 2.9 copy-start.9
  658.9 22.7 %collective-permute-start.12 = (f32[15,128,128]{2,1,0:T(8,128)S(1)}, f32[15,128,128]{2,1,0:T(8,128)S(1)}, u32[]{:S(2)}, u32[]{:S(2)}) collective-permute-start(f32[15,128,128]{2,1,0:T(8,128)S(1)} %get-tuple-element.104), channel_id=1, source_target_pairs={{0,2},{2,4},{4,6},{6,8},{8,10},{10,12},{12,14},{14,16},{16,18},{18... | collective-permute-start | bytes 2949128 | tf_op jit(solution)/shard_map/ppermute | solution.py:25
  662.0 23.5 %collective-permute-start.13 = (f32[15,128,128]{2,1,0:T(8,128)S(1)}, f32[15,128,128]{2,1,0:T(8,128)S(1)}, u32[]{:S(2)}, u32[]{:S(2)}) collective-permute-start(f32[15,128,128]{2,1,0:T(8,128)S(1)} %get-tuple-element.103), channel_id=1, source_target_pairs={{2,0},{4,2},{6,4},{8,6},{10,8},{12,10},{14,12},{16,14},{18,16},{20... | collective-permute-start | bytes 2949128 | tf_op jit(solution)/shard_map/ppermute | solution.py:25
  685.8 1.0 copy-start.3
  686.8 189.2 %all-reduce.11.cloned.1.call-start = ((), (), s32[]{:S(2)}) async-start(), calls=%async_computation.3 | async-start | bytes 2097152 | tf_op jit(solution)/shard_map/psum | solution.py:83
  723.7 24.1 %collective-permute-start.14 = (f32[15,128,128]{2,1,0:T(8,128)S(1)}, f32[15,128,128]{2,1,0:T(8,128)S(1)}, u32[]{:S(2)}, u32[]{:S(2)}) collective-permute-start(f32[15,128,128]{2,1,0:T(8,128)S(1)} %get-tuple-element.109), channel_id=1, source_target_pairs={{0,2},{2,4},{4,6},{6,8},{8,10},{10,12},{12,14},{14,16},{16,18},{18... | collective-permute-start | bytes 2949128 | tf_op jit(solution)/shard_map/ppermute | solution.py:14
  726.9 24.7 %collective-permute-start.15 = (f32[15,128,128]{2,1,0:T(8,128)S(1)}, f32[15,128,128]{2,1,0:T(8,128)S(1)}, u32[]{:S(2)}, u32[]{:S(2)}) collective-permute-start(f32[15,128,128]{2,1,0:T(8,128)S(1)} %get-tuple-element.110), channel_id=1, source_target_pairs={{2,0},{4,2},{6,4},{8,6},{10,8},{12,10},{14,12},{16,14},{18,16},{20... | collective-permute-start | bytes 2949128 | tf_op jit(solution)/shard_map/ppermute | solution.py:17
  760.3 2.9 copy-start.10
  812.9 22.7 %collective-permute-start.16 = (f32[15,128,128]{2,1,0:T(8,128)S(1)}, f32[15,128,128]{2,1,0:T(8,128)S(1)}, u32[]{:S(2)}, u32[]{:S(2)}) collective-permute-start(f32[15,128,128]{2,1,0:T(8,128)S(1)} %get-tuple-element.102), channel_id=1, source_target_pairs={{0,2},{2,4},{4,6},{6,8},{8,10},{10,12},{12,14},{14,16},{16,18},{18... | collective-permute-start | bytes 2949128 | tf_op jit(solution)/shard_map/ppermute | solution.py:25
  816.0 23.5 %collective-permute-start.17 = (f32[15,128,128]{2,1,0:T(8,128)S(1)}, f32[15,128,128]{2,1,0:T(8,128)S(1)}, u32[]{:S(2)}, u32[]{:S(2)}) collective-permute-start(f32[15,128,128]{2,1,0:T(8,128)S(1)} %get-tuple-element.101), channel_id=1, source_target_pairs={{2,0},{4,2},{6,4},{8,6},{10,8},{12,10},{14,12},{16,14},{18,16},{20... | collective-permute-start | bytes 2949128 | tf_op jit(solution)/shard_map/ppermute | solution.py:25
  839.8 1.0 copy-start.4
Sparse Core Ops, SparseCore 0:
  371.7 41.8 all-reduce.4
  532.6 35.0 all-reduce.6
  686.9 35.0 all-reduce.8
  840.9 35.0 all-reduce.10
where the time goes:
time: 898 us; the launch traced here: 885 us
  waiting for transfers between devices  299 us (33%)
  matrix products  255 us (28%)
  other arithmetic  243 us (27%)
  starting transfers between devices  44.1 us (5%)
  local copies, waits for them, and re-layouts  24.5 us (3%)
  between operations  14.3 us (2%)
    add x12, other arithmetic, make_band(): matrix = matrix + taps[lag] * (spacing == lag).astype(jnp.float32)  233 us
    psum x4, waiting for transfers between devices, per_device(): summed = lax.psum(total, 'view')  142 us
    dot_general x4, matrix products, per_device(): wide_total = jnp.einsum('vx,vxyz->xyz', cover_wide, spread, precision=hp)  138 us
    ppermute x8, waiting for transfers between devices, shifted(): return lax.ppermute(x, axis, pairs)  87.6 us
    ppermute x5, waiting for transfers between devices, with_halo(): lax.ppermute(lax.slice_in_dim(block, block.shape[dim] - width, None, axis...  57.7 us
    dot_general x4, matrix products, per_device(): spread = jnp.einsum('vxyz,vwx->vwyz', inner, x_spread, precision=hp)  46.6 us
    ppermute x8, starting transfers between devices, shifted(): return lax.ppermute(x, axis, pairs)  18.6 us
    dot_general x4, matrix products, per_device(): first = jnp.einsum('xyz,vwx->vwyz', padded, x_forward, precision=hp)  18.5 us
  transfers between devices with their start and end apart: 22, of which 18 were waited for; matrix products, arithmetic and copies ran while one was open for 29% of the time, Pallas kernels for 0%

commit v1 on v0

v1 whole, which is shorter than its diff:
```python
import jax
import jax.numpy as jnp
from jax import lax
from jax.experimental import pallas as pl
from jax.experimental.pallas import tpu as pltpu
from jax.sharding import PartitionSpec as P

ITERS = 4
TAPS = 31
REACH = 15
VIEWS = 6
W = 16
HALF = 64
EXT = 96
MID = 80
SLOTS = 48
NZ = 128
F32 = jnp.float32
BF16 = jnp.bfloat16
VMEM = pl.BlockSpec(memory_space=pltpu.VMEM)
SMEM = pl.BlockSpec(memory_space=pltpu.SMEM)


def split(x):
    high = x.astype(BF16)
    return high, (x - high.astype(F32)).astype(BF16)


def dot(a, b):
    return jnp.dot(a, b, preferred_element_type=F32)


def iota(shape, dim):
    return lax.broadcasted_iota(jnp.int32, shape, dim)


def plane_of(slot, core):
    middle = slot - REACH
    swapped = jnp.where(slot < REACH, slot + W, jnp.where(slot < REACH + W, middle, slot - 46))
    return jnp.where(core == 0, middle, swapped)


def row_of(j, core):
    first = jnp.where(j < 32, j + 32, jnp.where(j < 64, j - 32, j))
    second = jnp.where(j < 64, j + 64, j - 32)
    return jnp.where(core == 0, first, second)


def mid_row_of(j, core):
    return jnp.where((core == 1) & (j >= 64), j - 16, row_of(j, core))


def matrices_kernel(where, taps, cover, xf, xt, yf, yt, zf, zt):
    core, tile = where[0], where[1]

    def put(ref, lead, rows, value):
        high, low = split(value)
        ref[lead + (pl.ds(0, rows),)] = high
        ref[lead + (pl.ds(rows, rows),)] = low

    def select(view, axis, index):
        total = jnp.zeros(index.shape, F32)
        for k in range(TAPS):
            total = jnp.where(index == k, taps[(view * 3 + axis) * TAPS + k], total)
        return total

    shape = (VIEWS * W, 2 * SLOTS)
    slot = iota(shape, 1)
    slot = jnp.where(slot < SLOTS, slot, slot - SLOTS)
    plane = plane_of(slot, core)
    at = plane + W * tile
    fine = (slot < 46) & (at >= 0) & (at < 1024)
    row = iota(shape, 0)
    index = jnp.where(fine, plane - row % W + REACH, -1)
    total = jnp.zeros(shape, F32)
    for view in range(VIEWS):
        total = jnp.where(row // W == view, select(view, 0, index), total)
    put(xf, (), VIEWS * W, total)

    shape = (SLOTS, 2 * VIEWS * W)
    slot = iota(shape, 0)
    plane = plane_of(slot, 1 - core)
    at = plane + W * tile
    fine = (slot < 46) & (at >= 0) & (at < 1024)
    column = iota(shape, 1)
    column = jnp.where(column < VIEWS * W, column, column - VIEWS * W)
    index = jnp.where(fine, plane - column % W + REACH, -1)
    total = jnp.zeros(shape, F32)
    for view in range(VIEWS):
        covered = jnp.zeros((SLOTS, 2 * VIEWS * W), F32)
        for p in range(3 * W):
            covered = jnp.where(plane == p - W, cover[(p // W) * VIEWS * W + view * W + p % W], covered)
        total = jnp.where(column // W == view, select(view, 0, index) * covered, total)
    put(xt, (), SLOTS, total)

    def per_view(view, _):
        shape = (MID, 2 * EXT)
        j = iota(shape, 1)
        j = jnp.where(j < EXT, j, j - EXT)
        index = row_of(j, core) - mid_row_of(iota(shape, 0), core) + REACH
        put(yf, (view,), MID, select(view, 1, index))
        shape = (HALF, 2 * MID)
        j = iota(shape, 1)
        j = jnp.where(j < MID, j, j - MID)
        index = row_of(iota(shape, 0), core) - mid_row_of(j, core) + REACH
        put(yt, (view,), HALF, select(view, 1, index))
        difference = iota((NZ, NZ), 0) - iota((NZ, NZ), 1)
        for ref, sign in ((zf, 1), (zt, -1)):
            high, low = split(select(view, 2, sign * difference + REACH))
            for start in (0, NZ):
                ref[view, pl.ds(start, NZ), pl.ds(0, NZ)] = high
                ref[view, pl.ds(start, NZ), pl.ds(NZ, NZ)] = low
        return 0

    lax.fori_loop(0, VIEWS, per_view, 0)


def make_matrices(where, taps, cover):
    shapes = [
        (2 * VIEWS * W, 2 * SLOTS),
        (2 * SLOTS, 2 * VIEWS * W),
        (VIEWS, 2 * MID, 2 * EXT),
        (VIEWS, 2 * HALF, 2 * MID),
        (VIEWS, 2 * NZ, 2 * NZ),
        (VIEWS, 2 * NZ, 2 * NZ),
    ]
    return pl.pallas_call(
        matrices_kernel,
        out_shape=[jax.ShapeDtypeStruct(s, BF16) for s in shapes],
        in_specs=[SMEM, SMEM, SMEM],
        out_specs=[VMEM] * 6,
        compiler_params=pltpu.CompilerParams(vmem_limit_bytes=24 << 20),
        cost_estimate=pl.CostEstimate(flops=4_000_000, bytes_accessed=6_000_000, transcendentals=0),
        name="matrices",
    )(where, taps, cover)


def both(result):
    half = result.shape[0] // 2
    return result[:half] + result[half:]


def correct_kernel(first, own, second, other, data, xf, xt, yf, yt, zf, zt, out1, out_own, out2, ext, mid, wide):
    def place(source, slot, count):
        for i in range(count):
            ext[pl.ds((slot + i) * EXT, HALF)] = source[i]

    place(first, 0, 15)
    place(own, 15, 16)
    place(second, 31, 15)
    for i in range(46):
        ext[pl.ds(i * EXT + HALF, 32)] = other[i]
    for i in range(46, SLOTS):
        ext[pl.ds(i * EXT, EXT)] = jnp.zeros((EXT, NZ), F32)

    group = 4

    def forward_x(step, _):
        parts = [split(ext[pl.ds(step * group + i, SLOTS, stride=EXT)]) for i in range(group)]
        operand = jnp.concatenate(
            [jnp.concatenate([p[0] for p in parts], 1), jnp.concatenate([p[1] for p in parts], 1)], 0
        )
        result = both(dot(xf[...], operand))
        for i in range(group):
            mid[pl.ds(step * group + i, VIEWS * W, stride=EXT)] = result[:, i * NZ : (i + 1) * NZ]
        return 0

    lax.fori_loop(0, EXT // group, forward_x, 0)

    planes = 4

    def inner(step, _):
        view = step // (W // planes)
        start = pl.multiple_of(step * planes * EXT, 8)
        block = mid[pl.ds(start, planes * EXT)]
        result = dot(jnp.concatenate(split(block), 1), zf[view])
        block = result[:, :NZ] + result[:, NZ:]
        high, low = split(block)
        operand = jnp.concatenate(
            [jnp.concatenate([x[i * EXT : (i + 1) * EXT] for i in range(planes)], 1) for x in (high, low)], 0
        )
        blurred = both(dot(yf[view], operand))
        measured = jnp.concatenate([data[step * planes + i] for i in range(planes)], 1)
        high, low = split(measured / blurred)
        result = both(dot(yt[view], jnp.concatenate([high, low], 0)))
        block = jnp.concatenate([result[:, i * NZ : (i + 1) * NZ] for i in range(planes)], 0)
        result = dot(jnp.concatenate(split(block), 1), zt[view])
        block = result[:, :NZ] + result[:, NZ:]
        for i in range(planes):
            mid[pl.ds(start + i * EXT, HALF)] = block[i * HALF : (i + 1) * HALF]
        return 0

    lax.fori_loop(0, VIEWS * W // planes, inner, 0)

    def adjoint_x(step, _):
        parts = [split(mid[pl.ds(step * group + i, VIEWS * W, stride=EXT)]) for i in range(group)]
        operand = jnp.concatenate(
            [jnp.concatenate([p[0] for p in parts], 1), jnp.concatenate([p[1] for p in parts], 1)], 0
        )
        result = both(dot(xt[...], operand))
        for i in range(group):
            wide[pl.ds(step * group + i, SLOTS, stride=HALF)] = result[:, i * NZ : (i + 1) * NZ]
        return 0

    lax.fori_loop(0, HALF // group, adjoint_x, 0)

    for i in range(15):
        out1[i] = wide[pl.ds(i * HALF, HALF)]
        out2[i] = wide[pl.ds((i + 31) * HALF, HALF)]
    for i in range(16):
        out_own[i] = wide[pl.ds((i + 15) * HALF, HALF)]


def correct(first, own, second, other, data, matrices):
    shapes = [(15, HALF, NZ), (16, HALF, NZ), (15, HALF, NZ)]
    return pl.pallas_call(
        correct_kernel,
        out_shape=[jax.ShapeDtypeStruct(s, F32) for s in shapes],
        in_specs=[VMEM] * 11,
        out_specs=[VMEM] * 3,
        scratch_shapes=[
            pltpu.VMEM((SLOTS * EXT, NZ), F32),
            pltpu.VMEM((VIEWS * W * EXT, NZ), F32),
            pltpu.VMEM((SLOTS * HALF, NZ), F32),
        ],
        compiler_params=pltpu.CompilerParams(vmem_limit_bytes=40 << 20),
        cost_estimate=pl.CostEstimate(flops=5_000_000_000, bytes_accessed=16_000_000, transcendentals=0),
        name="correct",
    )(first, own, second, other, data, *matrices)


def update_kernel(where, keep, scale, current, total, from1, from2, new, send1, send2, work):
    core = where[0]
    work[...] = total[...]
    work[pl.ds(core, 15)] += from1[...]
    work[pl.ds(1 - core, 15)] += from2[...]
    for i in range(W):
        new[i] = current[i] * (work[i] + keep[i]) * scale[i]
    send1[...] = new[pl.ds(1 - core, 15)]
    send2[...] = new[pl.ds(core, 15)]


def update(where, keep, scale, current, total, from1, from2):
    shapes = [(16, HALF, NZ), (15, HALF, NZ), (15, HALF, NZ)]
    return pl.pallas_call(
        update_kernel,
        out_shape=[jax.ShapeDtypeStruct(s, F32) for s in shapes],
        in_specs=[SMEM] * 3 + [VMEM] * 4,
        out_specs=[VMEM] * 3,
        scratch_shapes=[pltpu.VMEM((16, HALF, NZ), F32)],
        compiler_params=pltpu.CompilerParams(vmem_limit_bytes=16 << 20),
        cost_estimate=pl.CostEstimate(flops=1_000_000, bytes_accessed=4_000_000, transcendentals=0),
        name="update",
    )(where, keep, scale, current, total, from1, from2)


def neighbours(x, up_core, tiles):
    pairs = []
    for t in range(tiles):
        pairs.append((2 * t + up_core, 2 * ((t + 1) % tiles) + up_core))
        pairs.append((2 * t + 1 - up_core, 2 * ((t - 1) % tiles) + 1 - up_core))
    return lax.ppermute(x, ("tile", "view"), pairs)


def swap(x):
    return lax.ppermute(x, "view", [(0, 1), (1, 0)])


def per_device(estimate, view_data, psf_taps, coverage):
    tiles = lax.axis_size("tile")
    core = lax.axis_index("view")
    tile = lax.axis_index("tile")
    zero = core == 0
    where = jnp.stack([core, tile]).astype(jnp.int32)

    near_rows = jnp.where(zero, estimate[:, 32:64], estimate[:, 64:96])
    far_rows = jnp.where(zero, estimate[:, 0:32], estimate[:, 96:128])
    current = jnp.concatenate([near_rows, far_rows], 1)
    send1 = jnp.where(zero, current[1:], current[:-1])
    send2 = jnp.where(zero, current[:-1], current[1:])

    def rows(who, near):
        low = jnp.where(who, view_data[:, :, 32:64], view_data[:, :, 64:96])
        high = jnp.where(who, view_data[:, :, 0:32], view_data[:, :, 96:128])
        other = jnp.where(who, view_data[:, :, 64:80], view_data[:, :, 48:64])
        return jnp.concatenate([low, high, other], 2)

    data = jnp.concatenate([rows(zero, True), swap(rows(~zero, True))], 0).reshape(VIEWS * W, MID, NZ)

    norm_taps = psf_taps / jnp.sum(psf_taps, axis=-1, keepdims=True)
    weights = coverage.astype(F32)
    mine = jnp.concatenate([norm_taps.reshape(-1), weights.reshape(-1)])
    theirs = swap(mine)
    count = norm_taps.size
    taps = jnp.concatenate([mine[:count], theirs[:count]])
    cover = jnp.concatenate([mine[count:], theirs[count:]])
    ring = [(i, (i + 1) % tiles) for i in range(tiles)]
    back = [(j, i) for i, j in ring]
    swapped = cover.reshape(2, -1)
    before = lax.ppermute(cover, "tile", ring)
    after = lax.ppermute(cover, "tile", back)
    seen = jnp.sum(cover.reshape(VIEWS, W), axis=0)
    keep = 1.0 - jnp.minimum(seen, 1.0)
    scale = 1.0 / jnp.maximum(seen, 1.0)
    matrices = make_matrices(where, taps, jnp.concatenate([before, cover, after]))

    for iteration in range(ITERS):
        first = neighbours(send1, 0, tiles)
        second = neighbours(send2, 1, tiles)
        other = swap(jnp.concatenate([second[:, :32], current[:, :32], first[:, :32]], 0))
        spread1, total, spread2 = correct(first, current, second, other, data, matrices)
        from1 = neighbours(spread1, 0, tiles)
        from2 = neighbours(spread2, 1, tiles)
        current, send1, send2 = update(where, keep, scale, current, total, from1, from2)

    theirs = swap(current)
    low = jnp.where(zero, current, theirs)
    high = jnp.where(zero, theirs, current)
    return jnp.concatenate([low[:, 32:], low[:, :32], high[:, :32], high[:, 32:]], 1)


def solution(mesh):
    return jax.shard_map(
        per_device,
        mesh=mesh,
        in_specs=(
            P("tile", None, None),
            P("view", "tile", None, None),
            P("view", None, None),
            P("view", "tile"),
        ),
        out_specs=P("tile", None, None),
        check_vma=False,
    )
```

time: 898 us -> 323 us (0.36); the launches traced: 885 us -> 322 us
  matrix products: 255 us -> 0 us
  other arithmetic: 243 us -> 11.5 us
  waiting for transfers between devices: 299 us -> 104 us
  Pallas kernels: 0 us -> 132 us
  starting transfers between devices: 44.1 us -> 72.4 us
  local copies, waits for them, and re-layouts: 24.5 us -> 2.72 us
  between operations: 14.3 us -> 0.39 us
    dot_general x28 -> x0, matrix products: 255 us -> none  [the longest x4 138 us: per_device(): wide_total = jnp.einsum('vx,vxyz->xyz', cover_wide, spread, precision=hp)]
    add x12 -> x0, other arithmetic: 233 us -> none  [make_band(): matrix = matrix + taps[lag] * (spacing == lag).astype(jnp.float32)]
    psum x4 -> x0, waiting for transfers between devices: 142 us -> none  [per_device(): summed = lax.psum(total, 'view')]
    pallas_call x0 -> x9, Pallas kernels: none -> 132 us  [the longest x4 122 us: correct(): pl.pallas_call(correct_kernel, out_shape=[jax.ShapeDtypeStruct(s, F32) fo...]
    ppermute x18 -> x25, waiting for transfers between devices: 157 us -> 104 us  [the longest x16 95.4 us: neighbours(): return lax.ppermute(x, ('tile', 'view'), pairs)]
    ppermute x18 -> x25, starting transfers between devices: 44 us -> 72.4 us  [the longest x16 50.7 us: neighbours(): return lax.ppermute(x, ('tile', 'view'), pairs)]
    slice x35 -> x13, local copies, waits for them, and re-layouts: 20.5 us -> 0.3 us  [the longest x1 0.07 us: per_device(): cover = jnp.concatenate([mine[count:], theirs[count:]])]
  transfers between devices with their start and end apart: 22 -> 25, of which waited for: 18 -> 21; matrix products, arithmetic and copies ran while one was open for 29% -> 1% of each run, Pallas kernels for 0% -> 2%
where the time goes in v1:
time: 323 us; the launch traced here: 322 us
  Pallas kernels  132 us (41%)
  waiting for transfers between devices  104 us (32%)
  starting transfers between devices  72.4 us (22%)
  other arithmetic  11.5 us (4%)
    pallas_call x4, Pallas kernels, correct(): pl.pallas_call(correct_kernel, out_shape=[jax.ShapeDtypeStruct(s, F32) fo...  122 us
    ppermute x16, waiting for transfers between devices, neighbours(): return lax.ppermute(x, ('tile', 'view'), pairs)  95.4 us
    ppermute x16, starting transfers between devices, neighbours(): return lax.ppermute(x, ('tile', 'view'), pairs)  50.7 us
    ppermute x7, starting transfers between devices, swap(): return lax.ppermute(x, 'view', [(0, 1), (1, 0)])  14.8 us
    ppermute x7, waiting for transfers between devices, swap(): return lax.ppermute(x, 'view', [(0, 1), (1, 0)])  7.51 us
    ppermute x1, starting transfers between devices, per_device(): after = lax.ppermute(cover, 'tile', back)  6.89 us
  transfers between devices with their start and end apart: 25, of which 21 were waited for; matrix products, arithmetic and copies ran while one was open for 1% of the time, Pallas kernels for 2%

profile of v1, /device:TPU:1, one launch (start us, length us, event | category | flops | bytes accessed | tf_op | source)
XLA Modules:
  0.0 322.5 jit_solution(10284216282320578871)
XLA Ops:
  0.0 3.1 slice_select_fusion.3
  3.1 2.1 slice_select_fusion.5
  5.2 1.4 pad_maximum_fusion.1
  6.6 1.4 collective-permute-start.4
  8.2 1.4 collective-permute-start.2
  9.6 7.2 %collective-permute-start.1 = (f32[15,64,128]{2,1,0:T(8,128)S(1)}, f32[15,64,128]{2,1,0:T(8,128)S(1)}, u32[]{:S(2)}, u32[]{:S(2)}) collective-permute-start(f32[15,64,128]{2,1,0:T(8,128)S(1)} %get-tuple-element.74), channel_id=1, source_target_pairs={{0,2},{1,127},{2,4},{3,1},{4,6},{5,3},{6,8},{7,5},{8,10},{9,7},{10... | collective-permute-start | bytes 1474568 | tf_op jit(solution)/shard_map/ppermute | solution.py:262
  17.4 5.6 %collective-permute-done.2.second = f32[15,64,128]{2,1,0:T(8,128)S(1)} collective-permute-done((f32[15,64,128]{2,1,0:T(8,128)S(1)}, f32[15,64,128]{2,1,0:T(8,128)S(1)}, u32[]{:S(2)}, u32[]{:S(2)}) %collective-permute-start.2) | collective-permute-done | bytes 491552 | tf_op jit(solution)/shard_map/ppermute | solution.py:262
  23.0 4.6 %collective-permute-done.1.first = f32[15,64,128]{2,1,0:T(8,128)S(1)} collective-permute-done((f32[15,64,128]{2,1,0:T(8,128)S(1)}, f32[15,64,128]{2,1,0:T(8,128)S(1)}, u32[]{:S(2)}, u32[]{:S(2)}) %collective-permute-start.1) | collective-permute-done | bytes 491552 | tf_op jit(solution)/shard_map/ppermute | solution.py:262
  27.6 3.8 %collective-permute-start.3 = (f32[46,32,128]{2,1,0:T(8,128)S(1)}, f32[46,32,128]{2,1,0:T(8,128)S(1)}, u32[]{:S(2)}, u32[]{:S(2)}) collective-permute-start(f32[46,32,128]{2,1,0:T(8,128)S(1)} %pad_maximum_fusion.3), channel_id=1, source_target_pairs={{0,1},{1,0},{2,3},{3,2},{4,5},{5,4},{6,7},{7,6},{8,9},{9,8},{10,11... | collective-permute-start | bytes 2261000 | tf_op jit(solution)/shard_map/ppermute | solution.py:266
  31.7 6.9 %collective-permute-start.6 = (f32[96]{0:T(128)S(1)}, f32[96]{0:T(128)S(1)}, u32[]{:S(2)}, u32[]{:S(2)}) collective-permute-start(f32[96]{0:T(128)S(1)} %pad_maximum_fusion.11), channel_id=1, source_target_pairs={{2,0},{4,2},{6,4},{8,6},{10,8},{12,10},{14,12},{16,14},{18,16},{20... | collective-permute-start | bytes 1160 | tf_op jit(solution)/shard_map/ppermute | solution.py:301
  39.6 5.7 %matrices.1 = (bf16[192,96]{1,0:T(8,128)(2,1)S(1)}, bf16[96,192]{1,0:T(8,128)(2,1)S(1)}, bf16[6,160,192]{2,1,0:T(8,128)(2,1)S(1)}, bf16[6,128,160]{2,1,0:T(8,128...) custom-call(s32[2]{0:T(128)S(1)} %pad_add_fusion.where, f32[558]{0:T(1024)S(1)} %pad_maximum_fusion.8.taps, ...), custom_call_target="tpu_custom_call" | custom-call | flops 4000000 | bytes 6000000 | tf_op jit(solution)/shard_map/matrices/pallas_call | solution.py:127
  45.3 2.9 pad_maximum_fusion
  48.3 30.5 %correct.4 = (f32[15,64,128]{2,1,0:T(8,128)S(1)}, f32[16,64,128]{2,1,0:T(8,128)S(1)}, f32[15,64,128]{2,1,0:T(8,128)S(1)}) custom-call(f32[15,64,128]{2,1,0:T(8,128)S(1)} %collective-permute-done.1.first, f32[16,64,128]{2,1,0:T(8,128)S(1)} %pad_maximum_fusion.7.own.current, f32[15,64,128]{2,1,0:T(8,128)S(1)} %collective-permute-done.2.second, ...), custom_call_target="tpu_custom_call" | custom-call | flops 5000000000 | bytes 16000000 | tf_op jit(solution)/shard_map/correct/pallas_call | solution.py:216
  78.8 7.0 %collective-permute-start.7 = (f32[15,64,128]{2,1,0:T(8,128)S(1)}, f32[15,64,128]{2,1,0:T(8,128)S(1)}, u32[]{:S(2)}, u32[]{:S(2)}) collective-permute-start(f32[15,64,128]{2,1,0:T(8,128)S(1)} %get-tuple-element.40), channel_id=1, source_target_pairs={{0,2},{1,127},{2,4},{3,1},{4,6},{5,3},{6,8},{7,5},{8,10},{9,7},{10... | collective-permute-start | bytes 1474568 | tf_op jit(solution)/shard_map/ppermute | solution.py:262
  85.9 8.8 %collective-permute-done.7.from1 = f32[15,64,128]{2,1,0:T(8,128)S(1)} collective-permute-done((f32[15,64,128]{2,1,0:T(8,128)S(1)}, f32[15,64,128]{2,1,0:T(8,128)S(1)}, u32[]{:S(2)}, u32[]{:S(2)}) %collective-permute-start.7) | collective-permute-done | bytes 491552 | tf_op jit(solution)/shard_map/ppermute | solution.py:262
  94.7 4.1 %collective-permute-done.8.from2 = f32[15,64,128]{2,1,0:T(8,128)S(1)} collective-permute-done((f32[15,64,128]{2,1,0:T(8,128)S(1)}, f32[15,64,128]{2,1,0:T(8,128)S(1)}, u32[]{:S(2)}, u32[]{:S(2)}) %collective-permute-start.8) | collective-permute-done | bytes 491552 | tf_op jit(solution)/shard_map/ppermute | solution.py:262
  99.7 6.9 %collective-permute-start.9 = (f32[15,64,128]{2,1,0:T(8,128)S(1)}, f32[15,64,128]{2,1,0:T(8,128)S(1)}, u32[]{:S(2)}, u32[]{:S(2)}) collective-permute-start(f32[15,64,128]{2,1,0:T(8,128)S(1)} %get-tuple-element.43), channel_id=1, source_target_pairs={{0,2},{1,127},{2,4},{3,1},{4,6},{5,3},{6,8},{7,5},{8,10},{9,7},{10... | collective-permute-start | bytes 1474568 | tf_op jit(solution)/shard_map/ppermute | solution.py:262
  106.6 6.2 %collective-permute-done.10.second = f32[15,64,128]{2,1,0:T(8,128)S(1)} collective-permute-done((f32[15,64,128]{2,1,0:T(8,128)S(1)}, f32[15,64,128]{2,1,0:T(8,128)S(1)}, u32[]{:S(2)}, u32[]{:S(2)}) %collective-permute-start.10) | collective-permute-done | bytes 491552 | tf_op jit(solution)/shard_map/ppermute | solution.py:262
  112.9 4.3 %collective-permute-done.9.first = f32[15,64,128]{2,1,0:T(8,128)S(1)} collective-permute-done((f32[15,64,128]{2,1,0:T(8,128)S(1)}, f32[15,64,128]{2,1,0:T(8,128)S(1)}, u32[]{:S(2)}, u32[]{:S(2)}) %collective-permute-start.9) | collective-permute-done | bytes 491552 | tf_op jit(solution)/shard_map/ppermute | solution.py:262
  117.2 3.1 collective-permute-start.11
  120.4 1.9 collective-permute-done.11.other
  122.3 1.1 copy-done.5
  123.4 1.0 copy-done.7
  124.4 30.5 %correct.5 = (f32[15,64,128]{2,1,0:T(8,128)S(1)}, f32[16,64,128]{2,1,0:T(8,128)S(1)}, f32[15,64,128]{2,1,0:T(8,128)S(1)}) custom-call(f32[15,64,128]{2,1,0:T(8,128)S(1)} %collective-permute-done.9.first, f32[16,64,128]{2,1,0:T(8,128)S(1)} %get-tuple-element.42.own.current, f32[15,64,128]{2,1,0:T(8,128)S(1)} %collective-permute-done.10.second, ...), custom_call_target="tpu_custom_call" | custom-call | flops 5000000000 | bytes 16000000 | tf_op jit(solution)/shard_map/correct/pallas_call | solution.py:216
  154.9 4.7 %collective-permute-start.12 = (f32[15,64,128]{2,1,0:T(8,128)S(1)}, f32[15,64,128]{2,1,0:T(8,128)S(1)}, u32[]{:S(2)}, u32[]{:S(2)}) collective-permute-start(f32[15,64,128]{2,1,0:T(8,128)S(1)} %get-tuple-element.46), channel_id=1, source_target_pairs={{0,2},{1,127},{2,4},{3,1},{4,6},{5,3},{6,8},{7,5},{8,10},{9,7},{10... | collective-permute-start | bytes 1474568 | tf_op jit(solution)/shard_map/ppermute | solution.py:262
  159.6 7.7 %collective-permute-done.12.from1 = f32[15,64,128]{2,1,0:T(8,128)S(1)} collective-permute-done((f32[15,64,128]{2,1,0:T(8,128)S(1)}, f32[15,64,128]{2,1,0:T(8,128)S(1)}, u32[]{:S(2)}, u32[]{:S(2)}) %collective-permute-start.12) | collective-permute-done | bytes 491552 | tf_op jit(solution)/shard_map/ppermute | solution.py:262
  167.3 6.9 %collective-permute-done.13.from2 = f32[15,64,128]{2,1,0:T(8,128)S(1)} collective-permute-done((f32[15,64,128]{2,1,0:T(8,128)S(1)}, f32[15,64,128]{2,1,0:T(8,128)S(1)}, u32[]{:S(2)}, u32[]{:S(2)}) %collective-permute-start.13) | collective-permute-done | bytes 491552 | tf_op jit(solution)/shard_map/ppermute | solution.py:262
  175.0 6.9 %collective-permute-start.14 = (f32[15,64,128]{2,1,0:T(8,128)S(1)}, f32[15,64,128]{2,1,0:T(8,128)S(1)}, u32[]{:S(2)}, u32[]{:S(2)}) collective-permute-start(f32[15,64,128]{2,1,0:T(8,128)S(1)} %get-tuple-element.49), channel_id=1, source_target_pairs={{0,2},{1,127},{2,4},{3,1},{4,6},{5,3},{6,8},{7,5},{8,10},{9,7},{10... | collective-permute-start | bytes 1474568 | tf_op jit(solution)/shard_map/ppermute | solution.py:262
  182.0 6.2 %collective-permute-done.15.second = f32[15,64,128]{2,1,0:T(8,128)S(1)} collective-permute-done((f32[15,64,128]{2,1,0:T(8,128)S(1)}, f32[15,64,128]{2,1,0:T(8,128)S(1)}, u32[]{:S(2)}, u32[]{:S(2)}) %collective-permute-start.15) | collective-permute-done | bytes 491552 | tf_op jit(solution)/shard_map/ppermute | solution.py:262
  188.2 2.9 collective-permute-done.14.first
  191.1 3.1 collective-permute-start.16
  194.3 1.9 collective-permute-done.16.other
  196.1 30.5 %correct.6 = (f32[15,64,128]{2,1,0:T(8,128)S(1)}, f32[16,64,128]{2,1,0:T(8,128)S(1)}, f32[15,64,128]{2,1,0:T(8,128)S(1)}) custom-call(f32[15,64,128]{2,1,0:T(8,128)S(1)} %collective-permute-done.14.first, f32[16,64,128]{2,1,0:T(8,128)S(1)} %get-tuple-element.48.own.current, f32[15,64,128]{2,1,0:T(8,128)S(1)} %collective-permute-done.15.second, ...), custom_call_target="tpu_custom_call" | custom-call | flops 5000000000 | bytes 16000000 | tf_op jit(solution)/shard_map/correct/pallas_call | solution.py:216
  226.6 4.7 %collective-permute-start.17 = (f32[15,64,128]{2,1,0:T(8,128)S(1)}, f32[15,64,128]{2,1,0:T(8,128)S(1)}, u32[]{:S(2)}, u32[]{:S(2)}) collective-permute-start(f32[15,64,128]{2,1,0:T(8,128)S(1)} %get-tuple-element.52), channel_id=1, source_target_pairs={{0,2},{1,127},{2,4},{3,1},{4,6},{5,3},{6,8},{7,5},{8,10},{9,7},{10... | collective-permute-start | bytes 1474568 | tf_op jit(solution)/shard_map/ppermute | solution.py:262
  231.3 7.7 %collective-permute-done.17.from1 = f32[15,64,128]{2,1,0:T(8,128)S(1)} collective-permute-done((f32[15,64,128]{2,1,0:T(8,128)S(1)}, f32[15,64,128]{2,1,0:T(8,128)S(1)}, u32[]{:S(2)}, u32[]{:S(2)}) %collective-permute-start.17) | collective-permute-done | bytes 491552 | tf_op jit(solution)/shard_map/ppermute | solution.py:262
  239.0 6.9 %collective-permute-done.18.from2 = f32[15,64,128]{2,1,0:T(8,128)S(1)} collective-permute-done((f32[15,64,128]{2,1,0:T(8,128)S(1)}, f32[15,64,128]{2,1,0:T(8,128)S(1)}, u32[]{:S(2)}, u32[]{:S(2)}) %collective-permute-start.18) | collective-permute-done | bytes 491552 | tf_op jit(solution)/shard_map/ppermute | solution.py:262
  246.8 6.9 %collective-permute-start.19 = (f32[15,64,128]{2,1,0:T(8,128)S(1)}, f32[15,64,128]{2,1,0:T(8,128)S(1)}, u32[]{:S(2)}, u32[]{:S(2)}) collective-permute-start(f32[15,64,128]{2,1,0:T(8,128)S(1)} %get-tuple-element.55), channel_id=1, source_target_pairs={{0,2},{1,127},{2,4},{3,1},{4,6},{5,3},{6,8},{7,5},{8,10},{9,7},{10... | collective-permute-start | bytes 1474568 | tf_op jit(solution)/shard_map/ppermute | solution.py:262
  253.7 6.2 %collective-permute-done.20.second = f32[15,64,128]{2,1,0:T(8,128)S(1)} collective-permute-done((f32[15,64,128]{2,1,0:T(8,128)S(1)}, f32[15,64,128]{2,1,0:T(8,128)S(1)}, u32[]{:S(2)}, u32[]{:S(2)}) %collective-permute-start.20) | collective-permute-done | bytes 491552 | tf_op jit(solution)/shard_map/ppermute | solution.py:262
  259.9 2.9 collective-permute-done.19.first
  262.9 3.1 collective-permute-start.21
  266.0 1.9 collective-permute-done.21.other
  267.9 30.5 %correct.7 = (f32[15,64,128]{2,1,0:T(8,128)S(1)}, f32[16,64,128]{2,1,0:T(8,128)S(1)}, f32[15,64,128]{2,1,0:T(8,128)S(1)}) custom-call(f32[15,64,128]{2,1,0:T(8,128)S(1)} %collective-permute-done.19.first, f32[16,64,128]{2,1,0:T(8,128)S(1)} %get-tuple-element.54.own.current, f32[15,64,128]{2,1,0:T(8,128)S(1)} %collective-permute-done.20.second, ...), custom_call_target="tpu_custom_call" | custom-call | flops 5000000000 | bytes 16000000 | tf_op jit(solution)/shard_map/correct/pallas_call | solution.py:216
  298.3 4.7 %collective-permute-start.22 = (f32[15,64,128]{2,1,0:T(8,128)S(1)}, f32[15,64,128]{2,1,0:T(8,128)S(1)}, u32[]{:S(2)}, u32[]{:S(2)}) collective-permute-start(f32[15,64,128]{2,1,0:T(8,128)S(1)} %get-tuple-element.58), channel_id=1, source_target_pairs={{0,2},{1,127},{2,4},{3,1},{4,6},{5,3},{6,8},{7,5},{8,10},{9,7},{10... | collective-permute-start | bytes 1474568 | tf_op jit(solution)/shard_map/ppermute | solution.py:262
  303.1 7.7 %collective-permute-done.22.from1 = f32[15,64,128]{2,1,0:T(8,128)S(1)} collective-permute-done((f32[15,64,128]{2,1,0:T(8,128)S(1)}, f32[15,64,128]{2,1,0:T(8,128)S(1)}, u32[]{:S(2)}, u32[]{:S(2)}) %collective-permute-start.22) | collective-permute-done | bytes 491552 | tf_op jit(solution)/shard_map/ppermute | solution.py:262
  310.7 6.9 %collective-permute-done.23.from2 = f32[15,64,128]{2,1,0:T(8,128)S(1)} collective-permute-done((f32[15,64,128]{2,1,0:T(8,128)S(1)}, f32[15,64,128]{2,1,0:T(8,128)S(1)}, u32[]{:S(2)}, u32[]{:S(2)}) %collective-permute-start.23) | collective-permute-done | bytes 491552 | tf_op jit(solution)/shard_map/ppermute | solution.py:262
  317.6 1.8 update.7
  319.4 1.9 collective-permute-done.24
  321.4 1.0 pad_maximum_fusion.2
  (82 shorter events, 5.4 us)
Async XLA Ops:
  3.1 4.9 %copy-start.13 = (f32[16,128,128]{2,1,0:T(8,128)S(1)}, f32[16,128,128]{2,1,0:T(8,128)}, u32[]{:S(2)}) copy-start(f32[16,128,128]{2,1,0:T(8,128)} %param.4) | copy-start | bytes 3145732
  5.2 11.6 %copy-start.14 = (s32[3,16]{1,0:T(4,128)S(1)}, s32[3,16]{1,0:T(4,128)}, u32[]{:S(2)}) copy-start(s32[3,16]{1,0:T(4,128)} %param.7) | copy-start | bytes 580
  5.2 11.7 %copy-start.15 = (f32[3,3,31]{2,1,0:T(4,128)S(1)}, f32[3,3,31]{2,1,0:T(4,128)}, u32[]{:S(2)}) copy-start(f32[3,3,31]{2,1,0:T(4,128)} %param.6) | copy-start | bytes 3352
  6.6 38.7 %collective-permute-start.4 = (f32[3,16,80,128]{3,2,1,0:T(8,128)}, f32[3,16,80,128]{3,2,1,0:T(8,128)}, u32[]{:S(2)}, u32[]{:S(2)}) collective-permute-start(f32[3,16,80,128]{3,2,1,0:T(8,128)} %pad_maximum_fusion.1), channel_id=1, source_target_pairs={{0,1},{1,0},{2,3},{3,2},{4,5},{5,4},{6,7},{7,6},{8,9},{9,8},{10,11... | collective-permute-start | bytes 5898248 | tf_op jit(solution)/shard_map/ppermute | solution.py:266
  8.2 14.8 %collective-permute-start.2 = (f32[15,64,128]{2,1,0:T(8,128)S(1)}, f32[15,64,128]{2,1,0:T(8,128)S(1)}, u32[]{:S(2)}, u32[]{:S(2)}) collective-permute-start(f32[15,64,128]{2,1,0:T(8,128)S(1)} %get-tuple-element.73), channel_id=1, source_target_pairs={{1,3},{0,126},{3,5},{2,0},{5,7},{4,2},{7,9},{6,4},{9,11},{8,6},{11... | collective-permute-start | bytes 1474568 | tf_op jit(solution)/shard_map/ppermute | solution.py:262
  9.6 17.9 %collective-permute-start.1 = (f32[15,64,128]{2,1,0:T(8,128)S(1)}, f32[15,64,128]{2,1,0:T(8,128)S(1)}, u32[]{:S(2)}, u32[]{:S(2)}) collective-permute-start(f32[15,64,128]{2,1,0:T(8,128)S(1)} %get-tuple-element.74), channel_id=1, source_target_pairs={{0,2},{1,127},{2,4},{3,1},{4,6},{5,3},{6,8},{7,5},{8,10},{9,7},{10... | collective-permute-start | bytes 1474568 | tf_op jit(solution)/shard_map/ppermute | solution.py:262
  17.1 14.4 %collective-permute-start = (f32[327]{0:T(512)S(1)}, f32[327]{0:T(512)S(1)}, u32[]{:S(2)}, u32[]{:S(2)}) collective-permute-start(f32[327]{0:T(512)S(1)} %pad_maximum_fusion.9), channel_id=1, source_target_pairs={{0,1},{1,0},{2,3},{3,2},{4,5},{5,4},{6,7},{7,6},{8,9},{9,8},{10,11... | collective-permute-start | bytes 3932 | tf_op jit(solution)/shard_map/ppermute | solution.py:266
  27.6 20.6 %collective-permute-start.3 = (f32[46,32,128]{2,1,0:T(8,128)S(1)}, f32[46,32,128]{2,1,0:T(8,128)S(1)}, u32[]{:S(2)}, u32[]{:S(2)}) collective-permute-start(f32[46,32,128]{2,1,0:T(8,128)S(1)} %pad_maximum_fusion.3), channel_id=1, source_target_pairs={{0,1},{1,0},{2,3},{3,2},{4,5},{5,4},{6,7},{7,6},{8,9},{9,8},{10,11... | collective-permute-start | bytes 2261000 | tf_op jit(solution)/shard_map/ppermute | solution.py:266
  31.7 7.8 %collective-permute-start.5 = (f32[96]{0:T(128)S(1)}, f32[96]{0:T(128)S(1)}, u32[]{:S(2)}, u32[]{:S(2)}) collective-permute-start(f32[96]{0:T(128)S(1)} %pad_maximum_fusion.11), channel_id=1, source_target_pairs={{0,2},{2,4},{4,6},{6,8},{8,10},{10,12},{12,14},{14,16},{16,18},{18... | collective-permute-start | bytes 1160 | tf_op jit(solution)/shard_map/ppermute | solution.py:300
  31.7 7.8 %collective-permute-start.6 = (f32[96]{0:T(128)S(1)}, f32[96]{0:T(128)S(1)}, u32[]{:S(2)}, u32[]{:S(2)}) collective-permute-start(f32[96]{0:T(128)S(1)} %pad_maximum_fusion.11), channel_id=1, source_target_pairs={{2,0},{4,2},{6,4},{8,6},{10,8},{12,10},{14,12},{16,14},{18,16},{20... | collective-permute-start | bytes 1160 | tf_op jit(solution)/shard_map/ppermute | solution.py:301
  45.3 3.0 copy-start.2
  45.3 3.0 copy-start.4
  45.3 3.0 copy-start.6
  45.3 3.0 copy-start.9
  45.3 3.0 copy-start.11
  48.2 30.5 %copy-start = (f32[6,16,80,128]{3,2,1,0:T(8,128)}, f32[6,16,80,128]{3,2,1,0:T(8,128)S(1)}, u32[]{:S(2)}) copy-start(f32[6,16,80,128]{3,2,1,0:T(8,128)S(1)} %pad_maximum_fusion) | copy-start | bytes 11796484
  78.8 15.9 %collective-permute-start.7 = (f32[15,64,128]{2,1,0:T(8,128)S(1)}, f32[15,64,128]{2,1,0:T(8,128)S(1)}, u32[]{:S(2)}, u32[]{:S(2)}) collective-permute-start(f32[15,64,128]{2,1,0:T(8,128)S(1)} %get-tuple-element.40), channel_id=1, source_target_pairs={{0,2},{1,127},{2,4},{3,1},{4,6},{5,3},{6,8},{7,5},{8,10},{9,7},{10... | collective-permute-start | bytes 1474568 | tf_op jit(solution)/shard_map/ppermute | solution.py:262
  85.7 13.1 %collective-permute-start.8 = (f32[15,64,128]{2,1,0:T(8,128)S(1)}, f32[15,64,128]{2,1,0:T(8,128)S(1)}, u32[]{:S(2)}, u32[]{:S(2)}) collective-permute-start(f32[15,64,128]{2,1,0:T(8,128)S(1)} %get-tuple-element.41), channel_id=1, source_target_pairs={{1,3},{0,126},{3,5},{2,0},{5,7},{4,2},{7,9},{6,4},{9,11},{8,6},{11... | collective-permute-start | bytes 1474568 | tf_op jit(solution)/shard_map/ppermute | solution.py:262
  85.8 36.4 %copy-start.1 = (f32[6,16,80,128]{3,2,1,0:T(8,128)S(1)}, f32[6,16,80,128]{3,2,1,0:T(8,128)}, u32[]{:S(2)}) copy-start(f32[6,16,80,128]{3,2,1,0:T(8,128)} %copy-done) | copy-start | bytes 11796484
  85.8 36.4 %copy-start.3 = (bf16[6,256,256]{2,1,0:T(8,128)(2,1)S(1)}, bf16[6,256,256]{2,1,0:T(8,128)(2,1)}, u32[]{:S(2)}) copy-start(bf16[6,256,256]{2,1,0:T(8,128)(2,1)} %copy-done.2) | copy-start | bytes 2359300
  85.9 36.4 %copy-start.10 = (bf16[192,96]{1,0:T(8,128)(2,1)S(1)}, bf16[192,96]{1,0:T(8,128)(2,1)}, u32[]{:S(2)}) copy-start(bf16[192,96]{1,0:T(8,128)(2,1)} %copy-done.9) | copy-start | bytes 110596
  85.9 36.4 %copy-start.12 = (bf16[96,192]{1,0:T(8,128)(2,1)S(1)}, bf16[96,192]{1,0:T(8,128)(2,1)}, u32[]{:S(2)}) copy-start(bf16[96,192]{1,0:T(8,128)(2,1)} %copy-done.11) | copy-start | bytes 110596
  99.7 13.2 %collective-permute-start.10 = (f32[15,64,128]{2,1,0:T(8,128)S(1)}, f32[15,64,128]{2,1,0:T(8,128)S(1)}, u32[]{:S(2)}, u32[]{:S(2)}) collective-permute-start(f32[15,64,128]{2,1,0:T(8,128)S(1)} %get-tuple-element.44), channel_id=1, source_target_pairs={{1,3},{0,126},{3,5},{2,0},{5,7},{4,2},{7,9},{6,4},{9,11},{8,6},{11... | collective-permute-start | bytes 1474568 | tf_op jit(solution)/shard_map/ppermute | solution.py:262
  99.7 17.4 %collective-permute-start.9 = (f32[15,64,128]{2,1,0:T(8,128)S(1)}, f32[15,64,128]{2,1,0:T(8,128)S(1)}, u32[]{:S(2)}, u32[]{:S(2)}) collective-permute-start(f32[15,64,128]{2,1,0:T(8,128)S(1)} %get-tuple-element.43), channel_id=1, source_target_pairs={{0,2},{1,127},{2,4},{3,1},{4,6},{5,3},{6,8},{7,5},{8,10},{9,7},{10... | collective-permute-start | bytes 1474568 | tf_op jit(solution)/shard_map/ppermute | solution.py:262
  117.2 5.0 %collective-permute-start.11 = (f32[46,32,128]{2,1,0:T(8,128)S(1)}, f32[46,32,128]{2,1,0:T(8,128)S(1)}, u32[]{:S(2)}, u32[]{:S(2)}) collective-permute-start(f32[46,32,128]{2,1,0:T(8,128)S(1)} %pad_maximum_fusion.4), channel_id=1, source_target_pairs={{0,1},{1,0},{2,3},{3,2},{4,5},{5,4},{6,7},{7,6},{8,9},{9,8},{10,11... | collective-permute-start | bytes 2261000 | tf_op jit(solution)/shard_map/ppermute | solution.py:266
  122.2 1.1 copy-start.5
  123.4 1.0 copy-start.7
  154.8 41.3 %copy-start.8 = (bf16[6,128,160]{2,1,0:T(8,128)(2,1)S(1)}, bf16[6,128,160]{2,1,0:T(8,128)(2,1)}, u32[]{:S(2)}) copy-start(bf16[6,128,160]{2,1,0:T(8,128)(2,1)} %copy-done.6) | copy-start | bytes 737284
  154.9 12.4 %collective-permute-start.12 = (f32[15,64,128]{2,1,0:T(8,128)S(1)}, f32[15,64,128]{2,1,0:T(8,128)S(1)}, u32[]{:S(2)}, u32[]{:S(2)}) collective-permute-start(f32[15,64,128]{2,1,0:T(8,128)S(1)} %get-tuple-element.46), channel_id=1, source_target_pairs={{0,2},{1,127},{2,4},{3,1},{4,6},{5,3},{6,8},{7,5},{8,10},{9,7},{10... | collective-permute-start | bytes 1474568 | tf_op jit(solution)/shard_map/ppermute | solution.py:262
  159.6 14.5 %collective-permute-start.13 = (f32[15,64,128]{2,1,0:T(8,128)S(1)}, f32[15,64,128]{2,1,0:T(8,128)S(1)}, u32[]{:S(2)}, u32[]{:S(2)}) collective-permute-start(f32[15,64,128]{2,1,0:T(8,128)S(1)} %get-tuple-element.47), channel_id=1, source_target_pairs={{1,3},{0,126},{3,5},{2,0},{5,7},{4,2},{7,9},{6,4},{9,11},{8,6},{11... | collective-permute-start | bytes 1474568 | tf_op jit(solution)/shard_map/ppermute | solution.py:262
  175.0 13.2 %collective-permute-start.15 = (f32[15,64,128]{2,1,0:T(8,128)S(1)}, f32[15,64,128]{2,1,0:T(8,128)S(1)}, u32[]{:S(2)}, u32[]{:S(2)}) collective-permute-start(f32[15,64,128]{2,1,0:T(8,128)S(1)} %get-tuple-element.50), channel_id=1, source_target_pairs={{1,3},{0,126},{3,5},{2,0},{5,7},{4,2},{7,9},{6,4},{9,11},{8,6},{11... | collective-permute-start | bytes 1474568 | tf_op jit(solution)/shard_map/ppermute | solution.py:262
  175.0 16.0 %collective-permute-start.14 = (f32[15,64,128]{2,1,0:T(8,128)S(1)}, f32[15,64,128]{2,1,0:T(8,128)S(1)}, u32[]{:S(2)}, u32[]{:S(2)}) collective-permute-start(f32[15,64,128]{2,1,0:T(8,128)S(1)} %get-tuple-element.49), channel_id=1, source_target_pairs={{0,2},{1,127},{2,4},{3,1},{4,6},{5,3},{6,8},{7,5},{8,10},{9,7},{10... | collective-permute-start | bytes 1474568 | tf_op jit(solution)/shard_map/ppermute | solution.py:262
  191.1 5.0 %collective-permute-start.16 = (f32[46,32,128]{2,1,0:T(8,128)S(1)}, f32[46,32,128]{2,1,0:T(8,128)S(1)}, u32[]{:S(2)}, u32[]{:S(2)}) collective-permute-start(f32[46,32,128]{2,1,0:T(8,128)S(1)} %pad_maximum_fusion.5), channel_id=1, source_target_pairs={{0,1},{1,0},{2,3},{3,2},{4,5},{5,4},{6,7},{7,6},{8,9},{9,8},{10,11... | collective-permute-start | bytes 2261000 | tf_op jit(solution)/shard_map/ppermute | solution.py:266
  226.6 12.4 %collective-permute-start.17 = (f32[15,64,128]{2,1,0:T(8,128)S(1)}, f32[15,64,128]{2,1,0:T(8,128)S(1)}, u32[]{:S(2)}, u32[]{:S(2)}) collective-permute-start(f32[15,64,128]{2,1,0:T(8,128)S(1)} %get-tuple-element.52), channel_id=1, source_target_pairs={{0,2},{1,127},{2,4},{3,1},{4,6},{5,3},{6,8},{7,5},{8,10},{9,7},{10... | collective-permute-start | bytes 1474568 | tf_op jit(solution)/shard_map/ppermute | solution.py:262
  231.3 14.6 %collective-permute-start.18 = (f32[15,64,128]{2,1,0:T(8,128)S(1)}, f32[15,64,128]{2,1,0:T(8,128)S(1)}, u32[]{:S(2)}, u32[]{:S(2)}) collective-permute-start(f32[15,64,128]{2,1,0:T(8,128)S(1)} %get-tuple-element.53), channel_id=1, source_target_pairs={{1,3},{0,126},{3,5},{2,0},{5,7},{4,2},{7,9},{6,4},{9,11},{8,6},{11... | collective-permute-start | bytes 1474568 | tf_op jit(solution)/shard_map/ppermute | solution.py:262
  246.7 13.2 %collective-permute-start.20 = (f32[15,64,128]{2,1,0:T(8,128)S(1)}, f32[15,64,128]{2,1,0:T(8,128)S(1)}, u32[]{:S(2)}, u32[]{:S(2)}) collective-permute-start(f32[15,64,128]{2,1,0:T(8,128)S(1)} %get-tuple-element.56), channel_id=1, source_target_pairs={{1,3},{0,126},{3,5},{2,0},{5,7},{4,2},{7,9},{6,4},{9,11},{8,6},{11... | collective-permute-start | bytes 1474568 | tf_op jit(solution)/shard_map/ppermute | solution.py:262
  246.8 16.0 %collective-permute-start.19 = (f32[15,64,128]{2,1,0:T(8,128)S(1)}, f32[15,64,128]{2,1,0:T(8,128)S(1)}, u32[]{:S(2)}, u32[]{:S(2)}) collective-permute-start(f32[15,64,128]{2,1,0:T(8,128)S(1)} %get-tuple-element.55), channel_id=1, source_target_pairs={{0,2},{1,127},{2,4},{3,1},{4,6},{5,3},{6,8},{7,5},{8,10},{9,7},{10... | collective-permute-start | bytes 1474568 | tf_op jit(solution)/shard_map/ppermute | solution.py:262
  262.9 5.0 %collective-permute-start.21 = (f32[46,32,128]{2,1,0:T(8,128)S(1)}, f32[46,32,128]{2,1,0:T(8,128)S(1)}, u32[]{:S(2)}, u32[]{:S(2)}) collective-permute-start(f32[46,32,128]{2,1,0:T(8,128)S(1)} %pad_maximum_fusion.6), channel_id=1, source_target_pairs={{0,1},{1,0},{2,3},{3,2},{4,5},{5,4},{6,7},{7,6},{8,9},{9,8},{10,11... | collective-permute-start | bytes 2261000 | tf_op jit(solution)/shard_map/ppermute | solution.py:266
  298.3 12.4 %collective-permute-start.22 = (f32[15,64,128]{2,1,0:T(8,128)S(1)}, f32[15,64,128]{2,1,0:T(8,128)S(1)}, u32[]{:S(2)}, u32[]{:S(2)}) collective-permute-start(f32[15,64,128]{2,1,0:T(8,128)S(1)} %get-tuple-element.58), channel_id=1, source_target_pairs={{0,2},{1,127},{2,4},{3,1},{4,6},{5,3},{6,8},{7,5},{8,10},{9,7},{10... | collective-permute-start | bytes 1474568 | tf_op jit(solution)/shard_map/ppermute | solution.py:262
  303.1 14.6 %collective-permute-start.23 = (f32[15,64,128]{2,1,0:T(8,128)S(1)}, f32[15,64,128]{2,1,0:T(8,128)S(1)}, u32[]{:S(2)}, u32[]{:S(2)}) collective-permute-start(f32[15,64,128]{2,1,0:T(8,128)S(1)} %get-tuple-element.59), channel_id=1, source_target_pairs={{1,3},{0,126},{3,5},{2,0},{5,7},{4,2},{7,9},{6,4},{9,11},{8,6},{11... | collective-permute-start | bytes 1474568 | tf_op jit(solution)/shard_map/ppermute | solution.py:262
  319.4 1.9 collective-permute-start.24

commit v2 on v1

v2 whole, which is shorter than its diff:
```python
import jax
import jax.numpy as jnp
from jax import lax
from jax.experimental import pallas as pl
from jax.experimental.pallas import tpu as pltpu
from jax.sharding import PartitionSpec as P

ITERS = 4
TAPS = 31
REACH = 15
VIEWS = 6
W = 16
HALF = 64
EXT = 96
MID = 80
SLOTS = 48
NZ = 128
OWN_STEP = 65
OTHER_STEP = 33
F32 = jnp.float32
BF16 = jnp.bfloat16
VMEM = pl.BlockSpec(memory_space=pltpu.VMEM)
SMEM = pl.BlockSpec(memory_space=pltpu.SMEM)


def split(x):
    high = x.astype(BF16)
    return high, (x - high.astype(F32)).astype(BF16)


def dot(a, b):
    return jnp.dot(a, b, preferred_element_type=F32)


def iota(shape, dim):
    return lax.broadcasted_iota(jnp.int32, shape, dim)


def plane_of(slot, core):
    middle = slot - REACH
    swapped = jnp.where(slot < REACH, slot + W, jnp.where(slot < REACH + W, middle, slot - 46))
    return jnp.where(core == 0, middle, swapped)


def row_of(j, core):
    first = jnp.where(j < 32, j + 32, jnp.where(j < 64, j - 32, j))
    second = jnp.where(j < 64, j + 64, j - 32)
    return jnp.where(core == 0, first, second)


def mid_row_of(j, core):
    return jnp.where((core == 1) & (j >= 64), j - 16, row_of(j, core))


def put(ref, lead, rows, value):
    high, low = split(value)
    ref[lead + (pl.ds(0, rows),)] = high
    ref[lead + (pl.ds(rows, rows),)] = low


def select(taps, view, axis, index):
    total = jnp.zeros(index.shape, F32)
    for k in range(TAPS):
        total = jnp.where(index == k, taps[(view * 3 + axis) * TAPS + k], total)
    return total


def in_grid(slot, plane, tile):
    at = plane + W * tile
    return (slot < 46) & (at >= 0) & (at < 1024)


def matrices_kernel(where, taps, xf, yf, yt, zf, zt):
    core, tile = where[0], where[1]

    shape = (VIEWS * W, 2 * SLOTS)
    slot = iota(shape, 1)
    slot = jnp.where(slot < SLOTS, slot, slot - SLOTS)
    plane = plane_of(slot, core)
    row = iota(shape, 0)
    index = jnp.where(in_grid(slot, plane, tile), plane - row % W + REACH, -1)
    total = jnp.zeros(shape, F32)
    for view in range(VIEWS):
        total = jnp.where(row // W == view, select(taps, view, 0, index), total)
    put(xf, (), VIEWS * W, total)

    def per_view(view, _):
        shape = (MID, 2 * EXT)
        j = iota(shape, 1)
        j = jnp.where(j < EXT, j, j - EXT)
        index = row_of(j, core) - mid_row_of(iota(shape, 0), core) + REACH
        put(yf, (view,), MID, select(taps, view, 1, index))
        shape = (HALF, 2 * MID)
        j = iota(shape, 1)
        j = jnp.where(j < MID, j, j - MID)
        index = row_of(iota(shape, 0), core) - mid_row_of(j, core) + REACH
        put(yt, (view,), HALF, select(taps, view, 1, index))
        difference = iota((NZ, NZ), 0) - iota((NZ, NZ), 1)
        for ref, sign in ((zf, 1), (zt, -1)):
            high, low = split(select(taps, view, 2, sign * difference + REACH))
            for start in (0, NZ):
                ref[view, pl.ds(start, NZ), pl.ds(0, NZ)] = high
                ref[view, pl.ds(start, NZ), pl.ds(NZ, NZ)] = low
        return 0

    lax.fori_loop(0, VIEWS, per_view, 0)


def make_matrices(where, taps):
    shapes = [
        (2 * VIEWS * W, 2 * SLOTS),
        (VIEWS, 2 * MID, 2 * EXT),
        (VIEWS, 2 * HALF, 2 * MID),
        (VIEWS, 2 * NZ, 2 * NZ),
        (VIEWS, 2 * NZ, 2 * NZ),
    ]
    return pl.pallas_call(
        matrices_kernel,
        out_shape=[jax.ShapeDtypeStruct(s, BF16) for s in shapes],
        in_specs=[SMEM, SMEM],
        out_specs=[VMEM] * 5,
        compiler_params=pltpu.CompilerParams(vmem_limit_bytes=6 << 20),
        cost_estimate=pl.CostEstimate(flops=6_000_000_000, bytes_accessed=6_000_000, transcendentals=0),
        name="matrices",
    )(where, taps)


def cover_kernel(where, taps, cover, xt):
    core, tile = where[0], where[1]
    shape = (SLOTS, 2 * VIEWS * W)
    slot = iota(shape, 0)
    plane = plane_of(slot, 1 - core)
    column = iota(shape, 1)
    column = jnp.where(column < VIEWS * W, column, column - VIEWS * W)
    index = jnp.where(in_grid(slot, plane, tile), plane - column % W + REACH, -1)
    total = jnp.zeros(shape, F32)
    for view in range(VIEWS):
        covered = jnp.zeros((SLOTS, 2 * VIEWS * W), F32)
        for p in range(3 * W):
            covered = jnp.where(plane == p - W, cover[(p // W) * VIEWS * W + view * W + p % W], covered)
        total = jnp.where(column // W == view, select(taps, view, 0, index) * covered, total)
    put(xt, (), SLOTS, total)


def cover_matrix(where, taps, cover):
    return pl.pallas_call(
        cover_kernel,
        out_shape=jax.ShapeDtypeStruct((2 * SLOTS, 2 * VIEWS * W), BF16),
        in_specs=[SMEM, SMEM, SMEM],
        out_specs=VMEM,
        compiler_params=pltpu.CompilerParams(vmem_limit_bytes=2 << 20),
        cost_estimate=pl.CostEstimate(flops=2_000_000_000, bytes_accessed=1_000_000, transcendentals=0),
        name="cover_matrix",
    )(where, taps, cover)


def both(result):
    half = result.shape[0] // 2
    return result[:half] + result[half:]


def pair(result):
    return result[:, :NZ] + result[:, NZ:]


def beside(blocks):
    return jnp.concatenate(blocks, 1)


def along_x(source, target, matrix, rows, taken, given, source_step, target_step):
    group = 16

    def body(step, _):
        parts = [split(source[pl.ds(step * group + i, taken, stride=source_step)]) for i in range(group)]
        operand = jnp.concatenate([beside([p[0] for p in parts]), beside([p[1] for p in parts])], 0)
        result = both(dot(matrix[...], operand))
        for i in range(group):
            target[pl.ds(step * group + i, given, stride=target_step)] = result[:, i * NZ : (i + 1) * NZ]
        return 0

    lax.fori_loop(0, rows // group, body, 0)


def place(ext, step, rows, sources):
    slot = 0
    for source in sources:
        for i in range(source.shape[0]):
            ext[pl.ds(slot * step, rows)] = source[i, pl.ds(0, rows)]
            slot += 1
    while slot < SLOTS:
        ext[pl.ds(slot * step, rows)] = jnp.zeros((rows, NZ), F32)
        slot += 1


def own_kernel(first, own, second, xf, zf, out_high, out_low, ext, mid):
    place(ext, OWN_STEP, HALF, (first, own, second))
    along_x(ext, mid, xf, HALF, SLOTS, VIEWS * W, OWN_STEP, OWN_STEP)

    def along_z(view, _):
        start = pl.multiple_of(view * (W * OWN_STEP), 16)
        block = jnp.concatenate([mid[pl.ds(start + i * OWN_STEP, HALF)] for i in range(W)], 0)
        high, low = split(pair(dot(beside(split(block)), zf[view])))
        for i in range(W):
            out_high[view * W + i] = high[i * HALF : (i + 1) * HALF]
            out_low[view * W + i] = low[i * HALF : (i + 1) * HALF]
        return 0

    lax.fori_loop(0, VIEWS, along_z, 0, unroll=3)


def blur_own(first, own, second, xf, zf):
    return pl.pallas_call(
        own_kernel,
        out_shape=[jax.ShapeDtypeStruct((VIEWS * W, HALF, NZ), BF16)] * 2,
        in_specs=[VMEM] * 5,
        out_specs=[VMEM] * 2,
        scratch_shapes=[pltpu.VMEM((SLOTS * OWN_STEP, NZ), F32), pltpu.VMEM((VIEWS * W * OWN_STEP, NZ), F32)],
        compiler_params=pltpu.CompilerParams(vmem_limit_bytes=14 << 20),
        cost_estimate=pl.CostEstimate(flops=20_000_000_000, bytes_accessed=6_000_000, transcendentals=0),
        name="blur_own",
    )(first, own, second, xf, zf)


def correct_kernel(
    own_high, own_low, other1, other2, other3, mine, theirs, xf, xt, yf, yt, zf, zt,
    out1, out_own, out2, ext, mid, back, wide,
):
    rest = EXT - HALF
    place(ext, OTHER_STEP, rest, (other1, other2, other3))
    along_x(ext, mid, xf, rest, SLOTS, VIEWS * W, OTHER_STEP, OTHER_STEP)

    def inner(data, base):
        def body(step, _):
            view = base + step
            start = pl.multiple_of(view * (W * OTHER_STEP), 16)
            block = jnp.concatenate([mid[pl.ds(start + i * OTHER_STEP, rest)] for i in range(W)], 0)
            parts = split(pair(dot(beside(split(block)), zf[view])))
            operand = jnp.concatenate(
                [
                    piece
                    for ref, part in zip((own_high, own_low), parts)
                    for piece in (
                        beside([ref[view * W + i] for i in range(W)]),
                        beside([part[i * rest : (i + 1) * rest] for i in range(W)]),
                    )
                ],
                0,
            )
            blurred = both(dot(yf[view], operand))
            measured = beside([data[step, i] for i in range(W)])
            result = both(dot(yt[view], jnp.concatenate(split(measured / blurred), 0)))
            block = jnp.concatenate([result[:, i * NZ : (i + 1) * NZ] for i in range(W)], 0)
            block = pair(dot(beside(split(block)), zt[view]))
            start = pl.multiple_of(view * (W * OWN_STEP), 16)
            for i in range(W):
                back[pl.ds(start + i * OWN_STEP, HALF)] = block[i * HALF : (i + 1) * HALF]
            return 0

        lax.fori_loop(0, VIEWS // 2, body, 0, unroll=3)

    inner(mine, 0)
    inner(theirs, VIEWS // 2)
    along_x(back, wide, xt, HALF, VIEWS * W, SLOTS, OWN_STEP, OWN_STEP)
    for i in range(15):
        out1[i] = wide[pl.ds(i * OWN_STEP, HALF)]
        out2[i] = wide[pl.ds((i + 31) * OWN_STEP, HALF)]
    for i in range(16):
        out_own[i] = wide[pl.ds((i + 15) * OWN_STEP, HALF)]


def correct(own_high, own_low, other1, other2, other3, mine, theirs, xf, xt, yf, yt, zf, zt):
    shapes = [(15, HALF, NZ), (16, HALF, NZ), (15, HALF, NZ)]
    return pl.pallas_call(
        correct_kernel,
        out_shape=[jax.ShapeDtypeStruct(s, F32) for s in shapes],
        in_specs=[VMEM] * 13,
        out_specs=[VMEM] * 3,
        scratch_shapes=[
            pltpu.VMEM((SLOTS * OTHER_STEP, NZ), F32),
            pltpu.VMEM((VIEWS * W * OTHER_STEP, NZ), F32),
            pltpu.VMEM((VIEWS * W * OWN_STEP, NZ), F32),
            pltpu.VMEM((SLOTS * OWN_STEP, NZ), F32),
        ],
        compiler_params=pltpu.CompilerParams(vmem_limit_bytes=28 << 20),
        cost_estimate=pl.CostEstimate(flops=4_000_000_000, bytes_accessed=16_000_000, transcendentals=0),
        name="correct",
    )(own_high, own_low, other1, other2, other3, mine, theirs, xf, xt, yf, yt, zf, zt)


def begin_kernel(where, estimate, current, send1, send2):
    core = where[0]
    near = pl.ds(pl.multiple_of(32 + 32 * core, 32), 32)
    far = pl.ds(pl.multiple_of(96 * core, 32), 32)
    for i in range(W):
        current[i, pl.ds(0, 32)] = estimate[i, near]
        current[i, pl.ds(32, 32)] = estimate[i, far]
    send1[...] = current[pl.ds(1 - core, 15)]
    send2[...] = current[pl.ds(core, 15)]


def begin(where, estimate):
    shapes = [(16, HALF, NZ), (15, HALF, NZ), (15, HALF, NZ)]
    return pl.pallas_call(
        begin_kernel,
        out_shape=[jax.ShapeDtypeStruct(s, F32) for s in shapes],
        in_specs=[SMEM, VMEM],
        out_specs=[VMEM] * 3,
        compiler_params=pltpu.CompilerParams(vmem_limit_bytes=6 << 20),
        cost_estimate=pl.CostEstimate(flops=1_000_000, bytes_accessed=4_000_000, transcendentals=0),
        name="begin",
    )(where, estimate)


def rows_kernel(where, data, mine, send):
    core = where[0]
    for ref, who in ((mine, core), (send, 1 - core)):
        for start, at, count in ((32 + 32 * who, 0, 32), (96 * who, 32, 32), (64 - 16 * who, 64, 16)):
            source = pl.ds(pl.multiple_of(start, 16), count)
            for view in range(VIEWS // 2):
                for i in range(W):
                    ref[view, i, pl.ds(at, count)] = data[view, i, source]


def rows(where, data):
    return pl.pallas_call(
        rows_kernel,
        out_shape=[jax.ShapeDtypeStruct((VIEWS // 2, W, MID, NZ), F32)] * 2,
        in_specs=[SMEM, VMEM],
        out_specs=[VMEM] * 2,
        compiler_params=pltpu.CompilerParams(vmem_limit_bytes=10 << 20),
        cost_estimate=pl.CostEstimate(flops=0, bytes_accessed=8_000_000, transcendentals=0),
        name="rows",
    )(where, data)


def update_kernel(where, keep, scale, current, total, from1, from2, new, send1, send2, work):
    core = where[0]
    work[...] = total[...]
    work[pl.ds(core, 15)] += from1[...]
    work[pl.ds(1 - core, 15)] += from2[...]
    for i in range(W):
        new[i] = current[i] * (work[i] + keep[i]) * scale[i]
    send1[...] = new[pl.ds(1 - core, 15)]
    send2[...] = new[pl.ds(core, 15)]


def update(where, keep, scale, current, total, from1, from2):
    shapes = [(16, HALF, NZ), (15, HALF, NZ), (15, HALF, NZ)]
    return pl.pallas_call(
        update_kernel,
        out_shape=[jax.ShapeDtypeStruct(s, F32) for s in shapes],
        in_specs=[SMEM] * 3 + [VMEM] * 4,
        out_specs=[VMEM] * 3,
        scratch_shapes=[pltpu.VMEM((16, HALF, NZ), F32)],
        compiler_params=pltpu.CompilerParams(vmem_limit_bytes=6 << 20),
        cost_estimate=pl.CostEstimate(flops=1_000_000, bytes_accessed=4_000_000, transcendentals=0),
        name="update",
    )(where, keep, scale, current, total, from1, from2)


def neighbours(x, up_core, tiles):
    pairs = []
    for t in range(tiles):
        pairs.append((2 * t + up_core, 2 * ((t + 1) % tiles) + up_core))
        pairs.append((2 * t + 1 - up_core, 2 * ((t - 1) % tiles) + 1 - up_core))
    return lax.ppermute(x, ("tile", "view"), pairs)


def swap(x):
    return lax.ppermute(x, "view", [(0, 1), (1, 0)])


def per_device(estimate, view_data, psf_taps, coverage):
    tiles = lax.axis_size("tile")
    core = lax.axis_index("view")
    tile = lax.axis_index("tile")
    where = jnp.stack([core, tile]).astype(jnp.int32)
    current, send1, send2 = begin(where, estimate)
    psf_taps, coverage, send1, send2 = lax.optimization_barrier((psf_taps, coverage, send1, send2))

    norm_taps = psf_taps / jnp.sum(psf_taps, axis=-1, keepdims=True)
    own = jnp.concatenate([norm_taps.reshape(-1), coverage.astype(F32).reshape(-1)])
    other, view_data = lax.optimization_barrier((swap(own), view_data))
    count = norm_taps.size
    taps = jnp.concatenate([own[:count], other[:count]])
    cover = jnp.concatenate([own[count:], other[count:]])
    ring = [(i, (i + 1) % tiles) for i in range(tiles)]
    before = lax.ppermute(cover, "tile", ring)
    after = lax.ppermute(cover, "tile", [(j, i) for i, j in ring])
    seen = jnp.sum(cover.reshape(VIEWS, W), axis=0)
    keep = 1.0 - jnp.minimum(seen, 1.0)
    scale = 1.0 / jnp.maximum(seen, 1.0)
    mine, theirs = rows(where, view_data)
    theirs = swap(theirs)
    xf, yf, yt, zf, zt = make_matrices(where, taps)
    xt = cover_matrix(where, taps, jnp.concatenate([before, cover, after]))

    for iteration in range(ITERS):
        first = neighbours(send1, 0, tiles)
        second = neighbours(send2, 1, tiles)
        high, low = blur_own(first, current, second, xf, zf)
        spread1, total, spread2 = correct(
            high, low, swap(second), swap(current), swap(first), mine, theirs, xf, xt, yf, yt, zf, zt
        )
        from1 = neighbours(spread1, 0, tiles)
        from2 = neighbours(spread2, 1, tiles)
        current, send1, send2 = update(where, keep, scale, current, total, from1, from2)

    other = swap(current)
    low = jnp.where(core == 0, current, other)
    high = jnp.where(core == 0, other, current)
    return jnp.concatenate([low[:, 32:], low[:, :32], high[:, :32], high[:, 32:]], 1)


def solution(mesh):
    return jax.shard_map(
        per_device,
        mesh=mesh,
        in_specs=(
            P("tile", None, None),
            P("view", "tile", None, None),
            P("view", None, None),
            P("view", "tile"),
        ),
        out_specs=P("tile", None, None),
        check_vma=False,
    )
```

time: 323 us -> 205 us (0.63)
  Pallas kernels: 132 us -> 45.5 us
  waiting for transfers between devices: 104 us -> 75.9 us
  other arithmetic: 11.5 us -> 3.1 us
  starting transfers between devices: 72.4 us -> 78.2 us
    pallas_call x4, Pallas kernels: 122 us -> 22.8 us  [correct(): pl.pallas_call(correct_kernel, out_shape=[jax.ShapeDtypeStruct(s, F32) fo...]
    ppermute x16, waiting for transfers between devices: 95.4 us -> 73.9 us  [neighbours(): return lax.ppermute(x, ('tile', 'view'), pairs)]
    pallas_call x0 -> x7, Pallas kernels: none -> 13.7 us  [the longest x4 10.7 us: blur_own(): pl.pallas_call(own_kernel, out_shape=[jax.ShapeDtypeStruct((VIEWS * W, HA...]
    ppermute x7 -> x15, starting transfers between devices: 14.8 us -> 20.7 us  [swap(): return lax.ppermute(x, 'view', [(0, 1), (1, 0)])]
    ppermute x7 -> x15, waiting for transfers between devices: 7.51 us -> 1.98 us  [swap(): return lax.ppermute(x, 'view', [(0, 1), (1, 0)])]
    select_n x5 -> x1, other arithmetic: 5.39 us -> 0.09 us  [per_device(): low = jnp.where(core == 0, current, other)]
    concatenate x11 -> x4, other arithmetic: 4.83 us -> 0.31 us  [the longest x1 0.08 us: per_device(): jnp.concatenate([norm_taps.reshape(-1), coverage.astype(F32).reshape(-1)])]
  transfers between devices with their start and end apart: 25 -> 33, of which waited for: 21 -> 14; matrix products, arithmetic and copies ran while one was open for 1% -> 0% of each run, Pallas kernels for 2% -> 9%
where the time goes in v2:
time: 205 us
  starting transfers between devices  78.2 us (38%)
  waiting for transfers between devices  75.9 us (37%)
  Pallas kernels  45.5 us (22%)
  other arithmetic  3.1 us (2%)
    ppermute x16, waiting for transfers between devices, neighbours(): return lax.ppermute(x, ('tile', 'view'), pairs)  73.9 us
    ppermute x16, starting transfers between devices, neighbours(): return lax.ppermute(x, ('tile', 'view'), pairs)  50.6 us
    pallas_call x4, Pallas kernels, correct(): pl.pallas_call(correct_kernel, out_shape=[jax.ShapeDtypeStruct(s, F32) fo...  22.8 us
    ppermute x15, starting transfers between devices, swap(): return lax.ppermute(x, 'view', [(0, 1), (1, 0)])  20.7 us
    pallas_call x4, Pallas kernels, blur_own(): pl.pallas_call(own_kernel, out_shape=[jax.ShapeDtypeStruct((VIEWS * W, HA...  10.7 us
    ppermute x1, starting transfers between devices, per_device(): after = lax.ppermute(cover, 'tile', [(j, i) for i, j in ring])  6.89 us
    pallas_call x1, Pallas kernels, make_matrices(): pl.pallas_call(matrices_kernel, out_shape=[jax.ShapeDtypeStruct(s, BF16)...  4.77 us
    pallas_call x4, Pallas kernels, update(): pl.pallas_call(update_kernel, out_shape=[jax.ShapeDtypeStruct(s, F32) for...  4.2 us
  transfers between devices with their start and end apart: 33, of which 14 were waited for; matrix products, arithmetic and copies ran while one was open for 0% of the time, Pallas kernels for 9%

profile of v2, /device:TPU:1, one launch (start us, length us, event | category | flops | bytes accessed | tf_op | source)
XLA Modules:
  0.0 204.8 jit_solution(563931731233424222)
XLA Ops:
  0.1 1.2 copy-done.1
  2.7 0.9 fusion.1
  3.7 1.4 collective-permute-start
  5.2 8.5 %collective-permute-start.1 = (f32[15,64,128]{2,1,0:T(8,128)S(1)}, f32[15,64,128]{2,1,0:T(8,128)S(1)}, u32[]{:S(2)}, u32[]{:S(2)}) collective-permute-start(f32[15,64,128]{2,1,0:T(8,128)S(1)} %get-tuple-element.57), channel_id=1, source_target_pairs={{0,2},{1,127},{2,4},{3,1},{4,6},{5,3},{6,8},{7,5},{8,10},{9,7},{10... | collective-permute-start | bytes 1474568 | tf_op jit(solution)/shard_map/ppermute | solution.py:366
  14.3 6.9 %collective-permute-start.8 = (f32[96]{0:T(128)S(1)}, f32[96]{0:T(128)S(1)}, u32[]{:S(2)}, u32[]{:S(2)}) collective-permute-start(f32[96]{0:T(128)S(1)} %pad_maximum_fusion.4), channel_id=1, source_target_pairs={{2,0},{4,2},{6,4},{8,6},{10,8},{12,10},{14,12},{16,14},{18,16},{20... | collective-permute-start | bytes 1160 | tf_op jit(solution)/shard_map/ppermute | solution.py:389
  21.2 4.8 %matrices.1 = (bf16[192,96]{1,0:T(8,128)(2,1)S(1)}, bf16[6,160,192]{2,1,0:T(8,128)(2,1)S(1)}, bf16[6,128,160]{2,1,0:T(8,128)(2,1)S(1)}, bf16[6,256,256]{2,1,0:T(8,128)(2,1)S(1)}, bf16[6,256,256]{2,1,0:T(8,128)(2,1)S(1)}) custom-call(s32[2]{0:T(128)S(1)} %pad_add_fusion.where, f32[558]{0:T(1024)S(1)} %pad_maximum_fusion.1.taps), custom_call_target="tpu_custom_call" | custom-call | flops 6000000000 | bytes 6000000 | tf_op jit(solution)/shard_map/matrices/pallas_call | solution.py:117
  26.1 0.8 rows.1
  27.7 1.6 cover_matrix.1.xt
  29.9 2.7 %blur_own.4 = (bf16[96,64,128]{2,1,0:T(8,128)(2,1)S(1)}, bf16[96,64,128]{2,1,0:T(8,128)(2,1)S(1)}) custom-call(f32[15,64,128]{2,1,0:T(8,128)S(1)} %collective-permute-done.1.first, f32[16,64,128]{2,1,0:T(8,128)S(1)} %get-tuple-element.56.own.current, f32[15,64,128]{2,1,0:T(8,128)S(1)} %collective-permute-done.2.second, ...), custom_call_target="tpu_custom_call" | custom-call | flops 20000000000 | bytes 6000000 | tf_op jit(solution)/shard_map/blur_own/pallas_call | solution.py:212
  32.7 5.7 %correct.4 = (f32[15,64,128]{2,1,0:T(8,128)S(1)}, f32[16,64,128]{2,1,0:T(8,128)S(1)}, f32[15,64,128]{2,1,0:T(8,128)S(1)}) custom-call(bf16[96,64,128]{2,1,0:T(8,128)(2,1)S(1)} %get-tuple-element.61.own_high, bf16[96,64,128]{2,1,0:T(8,128)(2,1)S(1)} %get-tuple-element.62.own_low, f32[15,64,128]{2,1,0:T(8,128)S(1)} %collective-permute-done.3.other1, ...), custom_call_target="tpu_custom_call" | custom-call | flops 4000000000 | bytes 16000000 | tf_op jit(solution)/shard_map/correct/pallas_call | solution.py:273
  38.5 6.9 %collective-permute-start.9 = (f32[15,64,128]{2,1,0:T(8,128)S(1)}, f32[15,64,128]{2,1,0:T(8,128)S(1)}, u32[]{:S(2)}, u32[]{:S(2)}) collective-permute-start(f32[15,64,128]{2,1,0:T(8,128)S(1)} %get-tuple-element.70), channel_id=1, source_target_pairs={{0,2},{1,127},{2,4},{3,1},{4,6},{5,3},{6,8},{7,5},{8,10},{9,7},{10... | collective-permute-start | bytes 1474568 | tf_op jit(solution)/shard_map/ppermute | solution.py:366
  45.5 6.1 %collective-permute-done.10.from2 = f32[15,64,128]{2,1,0:T(8,128)S(1)} collective-permute-done((f32[15,64,128]{2,1,0:T(8,128)S(1)}, f32[15,64,128]{2,1,0:T(8,128)S(1)}, u32[]{:S(2)}, u32[]{:S(2)}) %collective-permute-start.10) | collective-permute-done | bytes 491552 | tf_op jit(solution)/shard_map/ppermute | solution.py:366
  51.6 3.6 %collective-permute-done.9.from1 = f32[15,64,128]{2,1,0:T(8,128)S(1)} collective-permute-done((f32[15,64,128]{2,1,0:T(8,128)S(1)}, f32[15,64,128]{2,1,0:T(8,128)S(1)}, u32[]{:S(2)}, u32[]{:S(2)}) %collective-permute-start.9) | collective-permute-done | bytes 491552 | tf_op jit(solution)/shard_map/ppermute | solution.py:366
  55.1 0.8 update.4
  56.2 7.4 %collective-permute-start.11 = (f32[15,64,128]{2,1,0:T(8,128)S(1)}, f32[15,64,128]{2,1,0:T(8,128)S(1)}, u32[]{:S(2)}, u32[]{:S(2)}) collective-permute-start(f32[15,64,128]{2,1,0:T(8,128)S(1)} %get-tuple-element.73), channel_id=1, source_target_pairs={{0,2},{1,127},{2,4},{3,1},{4,6},{5,3},{6,8},{7,5},{8,10},{9,7},{10... | collective-permute-start | bytes 1474568 | tf_op jit(solution)/shard_map/ppermute | solution.py:366
  63.7 6.0 %collective-permute-done.12.second = f32[15,64,128]{2,1,0:T(8,128)S(1)} collective-permute-done((f32[15,64,128]{2,1,0:T(8,128)S(1)}, f32[15,64,128]{2,1,0:T(8,128)S(1)}, u32[]{:S(2)}, u32[]{:S(2)}) %collective-permute-start.12) | collective-permute-done | bytes 491552 | tf_op jit(solution)/shard_map/ppermute | solution.py:366
  69.7 4.8 %collective-permute-start.13 = (f32[15,64,128]{2,1,0:T(8,128)S(1)}, f32[15,64,128]{2,1,0:T(8,128)S(1)}, u32[]{:S(2)}, u32[]{:S(2)}) collective-permute-start(f32[15,64,128]{2,1,0:T(8,128)S(1)} %collective-permute-done.12.second), channel_id=1, source_target_pairs={{0,1},{1,0},{2,3},{3,2},{4,5},{5,4},{6,7},{7,6},{8,9},{9,8},{10,11... | collective-permute-start | bytes 1474568 | tf_op jit(solution)/shard_map/ppermute | solution.py:370
  74.6 2.9 %collective-permute-start.15 = (f32[15,64,128]{2,1,0:T(8,128)S(1)}, f32[15,64,128]{2,1,0:T(8,128)S(1)}, u32[]{:S(2)}, u32[]{:S(2)}) collective-permute-start(f32[15,64,128]{2,1,0:T(8,128)S(1)} %collective-permute-done.11.first), channel_id=1, source_target_pairs={{0,1},{1,0},{2,3},{3,2},{4,5},{5,4},{6,7},{7,6},{8,9},{9,8},{10,11... | collective-permute-start | bytes 1474568 | tf_op jit(solution)/shard_map/ppermute | solution.py:370
  77.5 2.7 %blur_own.5 = (bf16[96,64,128]{2,1,0:T(8,128)(2,1)S(1)}, bf16[96,64,128]{2,1,0:T(8,128)(2,1)S(1)}) custom-call(f32[15,64,128]{2,1,0:T(8,128)S(1)} %collective-permute-done.11.first, f32[16,64,128]{2,1,0:T(8,128)S(1)} %get-tuple-element.72.own.current, f32[15,64,128]{2,1,0:T(8,128)S(1)} %collective-permute-done.12.second, bf16[192,96]{1,0:T(8,128)(2,1)S(1)} %copy-done.13, ...), custom_call_target="tpu_custom_call" | custom-call | flops 20000000000 | bytes 6000000 | tf_op jit(solution)/shard_map/blur_own/pallas_call | solution.py:212
  80.2 5.7 %correct.5 = (f32[15,64,128]{2,1,0:T(8,128)S(1)}, f32[16,64,128]{2,1,0:T(8,128)S(1)}, f32[15,64,128]{2,1,0:T(8,128)S(1)}) custom-call(bf16[96,64,128]{2,1,0:T(8,128)(2,1)S(1)} %get-tuple-element.75.own_high, bf16[96,64,128]{2,1,0:T(8,128)(2,1)S(1)} %get-tuple-element.76.own_low, f32[15,64,128]{2,1,0:T(8,128)S(1)} %collective-permute-done.13.other1, ...), custom_call_target="tpu_custom_call" | custom-call | flops 4000000000 | bytes 16000000 | tf_op jit(solution)/shard_map/correct/pallas_call | solution.py:273
  86.0 4.9 %collective-permute-start.16 = (f32[15,64,128]{2,1,0:T(8,128)S(1)}, f32[15,64,128]{2,1,0:T(8,128)S(1)}, u32[]{:S(2)}, u32[]{:S(2)}) collective-permute-start(f32[15,64,128]{2,1,0:T(8,128)S(1)} %get-tuple-element.78), channel_id=1, source_target_pairs={{0,2},{1,127},{2,4},{3,1},{4,6},{5,3},{6,8},{7,5},{8,10},{9,7},{10... | collective-permute-start | bytes 1474568 | tf_op jit(solution)/shard_map/ppermute | solution.py:366
  90.8 8.1 %collective-permute-done.16.from1 = f32[15,64,128]{2,1,0:T(8,128)S(1)} collective-permute-done((f32[15,64,128]{2,1,0:T(8,128)S(1)}, f32[15,64,128]{2,1,0:T(8,128)S(1)}, u32[]{:S(2)}, u32[]{:S(2)}) %collective-permute-start.16) | collective-permute-done | bytes 491552 | tf_op jit(solution)/shard_map/ppermute | solution.py:366
  98.9 6.0 %collective-permute-done.17.from2 = f32[15,64,128]{2,1,0:T(8,128)S(1)} collective-permute-done((f32[15,64,128]{2,1,0:T(8,128)S(1)}, f32[15,64,128]{2,1,0:T(8,128)S(1)}, u32[]{:S(2)}, u32[]{:S(2)}) %collective-permute-start.17) | collective-permute-done | bytes 491552 | tf_op jit(solution)/shard_map/ppermute | solution.py:366
  104.9 0.8 update.5
  105.8 6.9 %collective-permute-start.18 = (f32[15,64,128]{2,1,0:T(8,128)S(1)}, f32[15,64,128]{2,1,0:T(8,128)S(1)}, u32[]{:S(2)}, u32[]{:S(2)}) collective-permute-start(f32[15,64,128]{2,1,0:T(8,128)S(1)} %get-tuple-element.81), channel_id=1, source_target_pairs={{0,2},{1,127},{2,4},{3,1},{4,6},{5,3},{6,8},{7,5},{8,10},{9,7},{10... | collective-permute-start | bytes 1474568 | tf_op jit(solution)/shard_map/ppermute | solution.py:366
  112.7 6.2 %collective-permute-done.19.second = f32[15,64,128]{2,1,0:T(8,128)S(1)} collective-permute-done((f32[15,64,128]{2,1,0:T(8,128)S(1)}, f32[15,64,128]{2,1,0:T(8,128)S(1)}, u32[]{:S(2)}, u32[]{:S(2)}) %collective-permute-start.19) | collective-permute-done | bytes 491552 | tf_op jit(solution)/shard_map/ppermute | solution.py:366
  118.9 2.3 %collective-permute-start.20 = (f32[15,64,128]{2,1,0:T(8,128)S(1)}, f32[15,64,128]{2,1,0:T(8,128)S(1)}, u32[]{:S(2)}, u32[]{:S(2)}) collective-permute-start(f32[15,64,128]{2,1,0:T(8,128)S(1)} %collective-permute-done.19.second), channel_id=1, source_target_pairs={{0,1},{1,0},{2,3},{3,2},{4,5},{5,4},{6,7},{7,6},{8,9},{9,8},{10,11... | collective-permute-start | bytes 1474568 | tf_op jit(solution)/shard_map/ppermute | solution.py:370
  121.2 1.1 collective-permute-done.18.first
  122.3 3.0 %collective-permute-start.22 = (f32[15,64,128]{2,1,0:T(8,128)S(1)}, f32[15,64,128]{2,1,0:T(8,128)S(1)}, u32[]{:S(2)}, u32[]{:S(2)}) collective-permute-start(f32[15,64,128]{2,1,0:T(8,128)S(1)} %collective-permute-done.18.first), channel_id=1, source_target_pairs={{0,1},{1,0},{2,3},{3,2},{4,5},{5,4},{6,7},{7,6},{8,9},{9,8},{10,11... | collective-permute-start | bytes 1474568 | tf_op jit(solution)/shard_map/ppermute | solution.py:370
  125.3 2.7 %blur_own.6 = (bf16[96,64,128]{2,1,0:T(8,128)(2,1)S(1)}, bf16[96,64,128]{2,1,0:T(8,128)(2,1)S(1)}) custom-call(f32[15,64,128]{2,1,0:T(8,128)S(1)} %collective-permute-done.18.first, f32[16,64,128]{2,1,0:T(8,128)S(1)} %get-tuple-element.80.own.current, f32[15,64,128]{2,1,0:T(8,128)S(1)} %collective-permute-done.19.second, bf16[192,96]{1,0:T(8,128)(2,1)S(1)} %copy-done.13, ...), custom_call_target="tpu_custom_call" | custom-call | flops 20000000000 | bytes 6000000 | tf_op jit(solution)/shard_map/blur_own/pallas_call | solution.py:212
  128.0 5.7 %correct.6 = (f32[15,64,128]{2,1,0:T(8,128)S(1)}, f32[16,64,128]{2,1,0:T(8,128)S(1)}, f32[15,64,128]{2,1,0:T(8,128)S(1)}) custom-call(bf16[96,64,128]{2,1,0:T(8,128)(2,1)S(1)} %get-tuple-element.83.own_high, bf16[96,64,128]{2,1,0:T(8,128)(2,1)S(1)} %get-tuple-element.84.own_low, f32[15,64,128]{2,1,0:T(8,128)S(1)} %collective-permute-done.20.other1, ...), custom_call_target="tpu_custom_call" | custom-call | flops 4000000000 | bytes 16000000 | tf_op jit(solution)/shard_map/correct/pallas_call | solution.py:273
  133.7 4.4 %collective-permute-start.23 = (f32[15,64,128]{2,1,0:T(8,128)S(1)}, f32[15,64,128]{2,1,0:T(8,128)S(1)}, u32[]{:S(2)}, u32[]{:S(2)}) collective-permute-start(f32[15,64,128]{2,1,0:T(8,128)S(1)} %get-tuple-element.86), channel_id=1, source_target_pairs={{0,2},{1,127},{2,4},{3,1},{4,6},{5,3},{6,8},{7,5},{8,10},{9,7},{10... | collective-permute-start | bytes 1474568 | tf_op jit(solution)/shard_map/ppermute | solution.py:366
  138.1 8.5 %collective-permute-done.23.from1 = f32[15,64,128]{2,1,0:T(8,128)S(1)} collective-permute-done((f32[15,64,128]{2,1,0:T(8,128)S(1)}, f32[15,64,128]{2,1,0:T(8,128)S(1)}, u32[]{:S(2)}, u32[]{:S(2)}) %collective-permute-start.23) | collective-permute-done | bytes 491552 | tf_op jit(solution)/shard_map/ppermute | solution.py:366
  146.6 6.1 %collective-permute-done.24.from2 = f32[15,64,128]{2,1,0:T(8,128)S(1)} collective-permute-done((f32[15,64,128]{2,1,0:T(8,128)S(1)}, f32[15,64,128]{2,1,0:T(8,128)S(1)}, u32[]{:S(2)}, u32[]{:S(2)}) %collective-permute-start.24) | collective-permute-done | bytes 491552 | tf_op jit(solution)/shard_map/ppermute | solution.py:366
  152.6 0.8 update.6
  153.6 6.9 %collective-permute-start.25 = (f32[15,64,128]{2,1,0:T(8,128)S(1)}, f32[15,64,128]{2,1,0:T(8,128)S(1)}, u32[]{:S(2)}, u32[]{:S(2)}) collective-permute-start(f32[15,64,128]{2,1,0:T(8,128)S(1)} %get-tuple-element.89), channel_id=1, source_target_pairs={{0,2},{1,127},{2,4},{3,1},{4,6},{5,3},{6,8},{7,5},{8,10},{9,7},{10... | collective-permute-start | bytes 1474568 | tf_op jit(solution)/shard_map/ppermute | solution.py:366
  160.4 6.2 %collective-permute-done.26.second = f32[15,64,128]{2,1,0:T(8,128)S(1)} collective-permute-done((f32[15,64,128]{2,1,0:T(8,128)S(1)}, f32[15,64,128]{2,1,0:T(8,128)S(1)}, u32[]{:S(2)}, u32[]{:S(2)}) %collective-permute-start.26) | collective-permute-done | bytes 491552 | tf_op jit(solution)/shard_map/ppermute | solution.py:366
  166.6 1.3 collective-permute-start.27
  168.0 1.6 collective-permute-done.25.first
  169.6 3.0 %collective-permute-start.29 = (f32[15,64,128]{2,1,0:T(8,128)S(1)}, f32[15,64,128]{2,1,0:T(8,128)S(1)}, u32[]{:S(2)}, u32[]{:S(2)}) collective-permute-start(f32[15,64,128]{2,1,0:T(8,128)S(1)} %collective-permute-done.25.first), channel_id=1, source_target_pairs={{0,1},{1,0},{2,3},{3,2},{4,5},{5,4},{6,7},{7,6},{8,9},{9,8},{10,11... | collective-permute-start | bytes 1474568 | tf_op jit(solution)/shard_map/ppermute | solution.py:370
  172.6 2.7 %blur_own.7 = (bf16[96,64,128]{2,1,0:T(8,128)(2,1)S(1)}, bf16[96,64,128]{2,1,0:T(8,128)(2,1)S(1)}) custom-call(f32[15,64,128]{2,1,0:T(8,128)S(1)} %collective-permute-done.25.first, f32[16,64,128]{2,1,0:T(8,128)S(1)} %get-tuple-element.88.own.current, f32[15,64,128]{2,1,0:T(8,128)S(1)} %collective-permute-done.26.second, bf16[192,96]{1,0:T(8,128)(2,1)S(1)} %copy-done.13, ...), custom_call_target="tpu_custom_call" | custom-call | flops 20000000000 | bytes 6000000 | tf_op jit(solution)/shard_map/blur_own/pallas_call | solution.py:212
  175.3 5.7 %correct.7 = (f32[15,64,128]{2,1,0:T(8,128)S(1)}, f32[16,64,128]{2,1,0:T(8,128)S(1)}, f32[15,64,128]{2,1,0:T(8,128)S(1)}) custom-call(bf16[96,64,128]{2,1,0:T(8,128)(2,1)S(1)} %get-tuple-element.91.own_high, bf16[96,64,128]{2,1,0:T(8,128)(2,1)S(1)} %get-tuple-element.92.own_low, f32[15,64,128]{2,1,0:T(8,128)S(1)} %collective-permute-done.27.other1, ...), custom_call_target="tpu_custom_call" | custom-call | flops 4000000000 | bytes 16000000 | tf_op jit(solution)/shard_map/correct/pallas_call | solution.py:273
  181.0 4.4 %collective-permute-start.30 = (f32[15,64,128]{2,1,0:T(8,128)S(1)}, f32[15,64,128]{2,1,0:T(8,128)S(1)}, u32[]{:S(2)}, u32[]{:S(2)}) collective-permute-start(f32[15,64,128]{2,1,0:T(8,128)S(1)} %get-tuple-element.94), channel_id=1, source_target_pairs={{0,2},{1,127},{2,4},{3,1},{4,6},{5,3},{6,8},{7,5},{8,10},{9,7},{10... | collective-permute-start | bytes 1474568 | tf_op jit(solution)/shard_map/ppermute | solution.py:366
  185.4 8.5 %collective-permute-done.30.from1 = f32[15,64,128]{2,1,0:T(8,128)S(1)} collective-permute-done((f32[15,64,128]{2,1,0:T(8,128)S(1)}, f32[15,64,128]{2,1,0:T(8,128)S(1)}, u32[]{:S(2)}, u32[]{:S(2)}) %collective-permute-start.30) | collective-permute-done | bytes 491552 | tf_op jit(solution)/shard_map/ppermute | solution.py:366
  193.9 6.0 %collective-permute-done.31.from2 = f32[15,64,128]{2,1,0:T(8,128)S(1)} collective-permute-done((f32[15,64,128]{2,1,0:T(8,128)S(1)}, f32[15,64,128]{2,1,0:T(8,128)S(1)}, u32[]{:S(2)}, u32[]{:S(2)}) %collective-permute-start.31) | collective-permute-done | bytes 491552 | tf_op jit(solution)/shard_map/ppermute | solution.py:366
  199.9 1.8 update.7
  201.7 1.9 collective-permute-done.32
  203.8 1.0 pad_maximum_fusion
  (85 shorter events, 4.7 us)
Async XLA Ops:
  3.7 10.4 %collective-permute-start = (f32[327]{0:T(512)S(1)}, f32[327]{0:T(512)S(1)}, u32[]{:S(2)}, u32[]{:S(2)}) collective-permute-start(f32[327]{0:T(512)S(1)} %pad_maximum_fusion.2), channel_id=1, source_target_pairs={{0,1},{1,0},{2,3},{3,2},{4,5},{5,4},{6,7},{7,6},{8,9},{9,8},{10,11... | collective-permute-start | bytes 3932 | tf_op jit(solution)/shard_map/ppermute | solution.py:370
  5.2 24.2 %collective-permute-start.1 = (f32[15,64,128]{2,1,0:T(8,128)S(1)}, f32[15,64,128]{2,1,0:T(8,128)S(1)}, u32[]{:S(2)}, u32[]{:S(2)}) collective-permute-start(f32[15,64,128]{2,1,0:T(8,128)S(1)} %get-tuple-element.57), channel_id=1, source_target_pairs={{0,2},{1,127},{2,4},{3,1},{4,6},{5,3},{6,8},{7,5},{8,10},{9,7},{10... | collective-permute-start | bytes 1474568 | tf_op jit(solution)/shard_map/ppermute | solution.py:366
  13.7 15.6 %collective-permute-start.2 = (f32[15,64,128]{2,1,0:T(8,128)S(1)}, f32[15,64,128]{2,1,0:T(8,128)S(1)}, u32[]{:S(2)}, u32[]{:S(2)}) collective-permute-start(f32[15,64,128]{2,1,0:T(8,128)S(1)} %get-tuple-element.58), channel_id=1, source_target_pairs={{1,3},{0,126},{3,5},{2,0},{5,7},{4,2},{7,9},{6,4},{9,11},{8,6},{11... | collective-permute-start | bytes 1474568 | tf_op jit(solution)/shard_map/ppermute | solution.py:366
  13.7 18.9 %collective-permute-start.4 = (f32[16,64,128]{2,1,0:T(8,128)S(1)}, f32[16,64,128]{2,1,0:T(8,128)S(1)}, u32[]{:S(2)}, u32[]{:S(2)}) collective-permute-start(f32[16,64,128]{2,1,0:T(8,128)S(1)} %get-tuple-element.56.own.current), channel_id=1, source_target_pairs={{0,1},{1,0},{2,3},{3,2},{4,5},{5,4},{6,7},{7,6},{8,9},{9,8},{10,11... | collective-permute-start | bytes 1572872 | tf_op jit(solution)/shard_map/ppermute | solution.py:370
  14.3 12.6 %collective-permute-start.7 = (f32[96]{0:T(128)S(1)}, f32[96]{0:T(128)S(1)}, u32[]{:S(2)}, u32[]{:S(2)}) collective-permute-start(f32[96]{0:T(128)S(1)} %pad_maximum_fusion.4), channel_id=1, source_target_pairs={{0,2},{2,4},{4,6},{6,8},{8,10},{10,12},{12,14},{14,16},{16,18},{18... | collective-permute-start | bytes 1160 | tf_op jit(solution)/shard_map/ppermute | solution.py:388
  14.3 13.3 %collective-permute-start.8 = (f32[96]{0:T(128)S(1)}, f32[96]{0:T(128)S(1)}, u32[]{:S(2)}, u32[]{:S(2)}) collective-permute-start(f32[96]{0:T(128)S(1)} %pad_maximum_fusion.4), channel_id=1, source_target_pairs={{2,0},{4,2},{6,4},{8,6},{10,8},{12,10},{14,12},{16,14},{18,16},{20... | collective-permute-start | bytes 1160 | tf_op jit(solution)/shard_map/ppermute | solution.py:389
  21.2 4.8 %copy-start = (f32[3,16,128,128]{3,2,1,0:T(8,128)S(1)}, f32[3,16,128,128]{3,2,1,0:T(8,128)}, u32[]{:S(2)}) copy-start(f32[3,16,128,128]{3,2,1,0:T(8,128)} %data) | copy-start | bytes 9437188
  26.0 6.6 %copy-start.6 = (bf16[6,256,256]{2,1,0:T(8,128)(2,1)}, bf16[6,256,256]{2,1,0:T(8,128)(2,1)S(1)}, u32[]{:S(2)}) copy-start(bf16[6,256,256]{2,1,0:T(8,128)(2,1)S(1)} %get-tuple-element.60.zf) | copy-start | bytes 2359300
  26.0 6.6 %copy-start.8 = (bf16[6,256,256]{2,1,0:T(8,128)(2,1)}, bf16[6,256,256]{2,1,0:T(8,128)(2,1)S(1)}, u32[]{:S(2)}) copy-start(bf16[6,256,256]{2,1,0:T(8,128)(2,1)S(1)} %get-tuple-element.68.zt) | copy-start | bytes 2359300
  26.0 6.6 %copy-start.10 = (bf16[6,128,160]{2,1,0:T(8,128)(2,1)}, bf16[6,128,160]{2,1,0:T(8,128)(2,1)S(1)}, u32[]{:S(2)}) copy-start(bf16[6,128,160]{2,1,0:T(8,128)(2,1)S(1)} %get-tuple-element.67.yt) | copy-start | bytes 737284
  26.1 6.6 %copy-start.12 = (bf16[192,96]{1,0:T(8,128)(2,1)}, bf16[192,96]{1,0:T(8,128)(2,1)S(1)}, u32[]{:S(2)}) copy-start(bf16[192,96]{1,0:T(8,128)(2,1)S(1)} %get-tuple-element.59.xf) | copy-start | bytes 110596
  26.9 5.8 %copy-start.2 = (f32[3,16,80,128]{3,2,1,0:T(8,128)}, f32[3,16,80,128]{3,2,1,0:T(8,128)S(1)}, u32[]{:S(2)}) copy-start(f32[3,16,80,128]{3,2,1,0:T(8,128)S(1)} %get-tuple-element.64.mine) | copy-start | bytes 5898244
  26.9 5.7 %collective-permute-start.6 = (f32[3,16,80,128]{3,2,1,0:T(8,128)S(1)}, f32[3,16,80,128]{3,2,1,0:T(8,128)S(1)}, u32[]{:S(2)}, u32[]{:S(2)}) collective-permute-start(f32[3,16,80,128]{3,2,1,0:T(8,128)S(1)} %get-tuple-element.65), channel_id=1, source_target_pairs={{0,1},{1,0},{2,3},{3,2},{4,5},{5,4},{6,7},{7,6},{8,9},{9,8},{10,11... | collective-permute-start | bytes 5898248 | tf_op jit(solution)/shard_map/ppermute | solution.py:370
  29.3 3.3 %collective-permute-start.3 = (f32[15,64,128]{2,1,0:T(8,128)S(1)}, f32[15,64,128]{2,1,0:T(8,128)S(1)}, u32[]{:S(2)}, u32[]{:S(2)}) collective-permute-start(f32[15,64,128]{2,1,0:T(8,128)S(1)} %collective-permute-done.2.second), channel_id=1, source_target_pairs={{0,1},{1,0},{2,3},{3,2},{4,5},{5,4},{6,7},{7,6},{8,9},{9,8},{10,11... | collective-permute-start | bytes 1474568 | tf_op jit(solution)/shard_map/ppermute | solution.py:370
  29.4 3.2 %collective-permute-start.5 = (f32[15,64,128]{2,1,0:T(8,128)S(1)}, f32[15,64,128]{2,1,0:T(8,128)S(1)}, u32[]{:S(2)}, u32[]{:S(2)}) collective-permute-start(f32[15,64,128]{2,1,0:T(8,128)S(1)} %collective-permute-done.1.first), channel_id=1, source_target_pairs={{0,1},{1,0},{2,3},{3,2},{4,5},{5,4},{6,7},{7,6},{8,9},{9,8},{10,11... | collective-permute-start | bytes 1474568 | tf_op jit(solution)/shard_map/ppermute | solution.py:370
  32.6 5.7 %copy-start.4 = (f32[3,16,80,128]{3,2,1,0:T(8,128)}, f32[3,16,80,128]{3,2,1,0:T(8,128)S(1)}, u32[]{:S(2)}) copy-start(f32[3,16,80,128]{3,2,1,0:T(8,128)S(1)} %collective-permute-done.6.theirs) | copy-start | bytes 5898244
  32.7 12.7 %copy-start.16 = (s32[3,16]{1,0:T(4,128)S(1)}, s32[3,16]{1,0:T(4,128)}, u32[]{:S(2)}) copy-start(s32[3,16]{1,0:T(4,128)} %param.7) | copy-start | bytes 580
  38.4 13.2 %collective-permute-start.10 = (f32[15,64,128]{2,1,0:T(8,128)S(1)}, f32[15,64,128]{2,1,0:T(8,128)S(1)}, u32[]{:S(2)}, u32[]{:S(2)}) collective-permute-start(f32[15,64,128]{2,1,0:T(8,128)S(1)} %get-tuple-element.71), channel_id=1, source_target_pairs={{1,3},{0,126},{3,5},{2,0},{5,7},{4,2},{7,9},{6,4},{9,11},{8,6},{11... | collective-permute-start | bytes 1474568 | tf_op jit(solution)/shard_map/ppermute | solution.py:366
  38.5 16.7 %collective-permute-start.9 = (f32[15,64,128]{2,1,0:T(8,128)S(1)}, f32[15,64,128]{2,1,0:T(8,128)S(1)}, u32[]{:S(2)}, u32[]{:S(2)}) collective-permute-start(f32[15,64,128]{2,1,0:T(8,128)S(1)} %get-tuple-element.70), channel_id=1, source_target_pairs={{0,2},{1,127},{2,4},{3,1},{4,6},{5,3},{6,8},{7,5},{8,10},{9,7},{10... | collective-permute-start | bytes 1474568 | tf_op jit(solution)/shard_map/ppermute | solution.py:366
  45.5 32.0 %copy-start.7 = (bf16[6,256,256]{2,1,0:T(8,128)(2,1)S(1)}, bf16[6,256,256]{2,1,0:T(8,128)(2,1)}, u32[]{:S(2)}) copy-start(bf16[6,256,256]{2,1,0:T(8,128)(2,1)} %copy-done.6) | copy-start | bytes 2359300
  45.5 32.0 %copy-start.13 = (bf16[192,96]{1,0:T(8,128)(2,1)S(1)}, bf16[192,96]{1,0:T(8,128)(2,1)}, u32[]{:S(2)}) copy-start(bf16[192,96]{1,0:T(8,128)(2,1)} %copy-done.12) | copy-start | bytes 110596
  55.9 13.8 %collective-permute-start.12 = (f32[15,64,128]{2,1,0:T(8,128)S(1)}, f32[15,64,128]{2,1,0:T(8,128)S(1)}, u32[]{:S(2)}, u32[]{:S(2)}) collective-permute-start(f32[15,64,128]{2,1,0:T(8,128)S(1)} %get-tuple-element.74), channel_id=1, source_target_pairs={{1,3},{0,126},{3,5},{2,0},{5,7},{4,2},{7,9},{6,4},{9,11},{8,6},{11... | collective-permute-start | bytes 1474568 | tf_op jit(solution)/shard_map/ppermute | solution.py:366
  56.2 18.4 %collective-permute-start.11 = (f32[15,64,128]{2,1,0:T(8,128)S(1)}, f32[15,64,128]{2,1,0:T(8,128)S(1)}, u32[]{:S(2)}, u32[]{:S(2)}) collective-permute-start(f32[15,64,128]{2,1,0:T(8,128)S(1)} %get-tuple-element.73), channel_id=1, source_target_pairs={{0,2},{1,127},{2,4},{3,1},{4,6},{5,3},{6,8},{7,5},{8,10},{9,7},{10... | collective-permute-start | bytes 1474568 | tf_op jit(solution)/shard_map/ppermute | solution.py:366
  63.6 16.6 %copy-start.3 = (f32[3,16,80,128]{3,2,1,0:T(8,128)S(1)}, f32[3,16,80,128]{3,2,1,0:T(8,128)}, u32[]{:S(2)}) copy-start(f32[3,16,80,128]{3,2,1,0:T(8,128)} %copy-done.2) | copy-start | bytes 5898244
  63.6 16.6 %copy-start.5 = (f32[3,16,80,128]{3,2,1,0:T(8,128)S(1)}, f32[3,16,80,128]{3,2,1,0:T(8,128)}, u32[]{:S(2)}) copy-start(f32[3,16,80,128]{3,2,1,0:T(8,128)} %copy-done.4) | copy-start | bytes 5898244
  63.6 16.6 %copy-start.9 = (bf16[6,256,256]{2,1,0:T(8,128)(2,1)S(1)}, bf16[6,256,256]{2,1,0:T(8,128)(2,1)}, u32[]{:S(2)}) copy-start(bf16[6,256,256]{2,1,0:T(8,128)(2,1)} %copy-done.8) | copy-start | bytes 2359300
  63.6 16.6 %copy-start.11 = (bf16[6,128,160]{2,1,0:T(8,128)(2,1)S(1)}, bf16[6,128,160]{2,1,0:T(8,128)(2,1)}, u32[]{:S(2)}) copy-start(bf16[6,128,160]{2,1,0:T(8,128)(2,1)} %copy-done.10) | copy-start | bytes 737284
  63.6 16.6 %copy-start.15 = (bf16[96,192]{1,0:T(8,128)(2,1)S(1)}, bf16[96,192]{1,0:T(8,128)(2,1)}, u32[]{:S(2)}) copy-start(bf16[96,192]{1,0:T(8,128)(2,1)} %copy-done.14) | copy-start | bytes 110596
  63.6 16.5 %collective-permute-start.14 = (f32[16,64,128]{2,1,0:T(8,128)S(1)}, f32[16,64,128]{2,1,0:T(8,128)S(1)}, u32[]{:S(2)}, u32[]{:S(2)}) collective-permute-start(f32[16,64,128]{2,1,0:T(8,128)S(1)} %get-tuple-element.72.own.current), channel_id=1, source_target_pairs={{0,1},{1,0},{2,3},{3,2},{4,5},{5,4},{6,7},{7,6},{8,9},{9,8},{10,11... | collective-permute-start | bytes 1572872 | tf_op jit(solution)/shard_map/ppermute | solution.py:370
  69.7 10.4 %collective-permute-start.13 = (f32[15,64,128]{2,1,0:T(8,128)S(1)}, f32[15,64,128]{2,1,0:T(8,128)S(1)}, u32[]{:S(2)}, u32[]{:S(2)}) collective-permute-start(f32[15,64,128]{2,1,0:T(8,128)S(1)} %collective-permute-done.12.second), channel_id=1, source_target_pairs={{0,1},{1,0},{2,3},{3,2},{4,5},{5,4},{6,7},{7,6},{8,9},{9,8},{10,11... | collective-permute-start | bytes 1474568 | tf_op jit(solution)/shard_map/ppermute | solution.py:370
  74.6 5.6 %collective-permute-start.15 = (f32[15,64,128]{2,1,0:T(8,128)S(1)}, f32[15,64,128]{2,1,0:T(8,128)S(1)}, u32[]{:S(2)}, u32[]{:S(2)}) collective-permute-start(f32[15,64,128]{2,1,0:T(8,128)S(1)} %collective-permute-done.11.first), channel_id=1, source_target_pairs={{0,1},{1,0},{2,3},{3,2},{4,5},{5,4},{6,7},{7,6},{8,9},{9,8},{10,11... | collective-permute-start | bytes 1474568 | tf_op jit(solution)/shard_map/ppermute | solution.py:370
  86.0 13.0 %collective-permute-start.16 = (f32[15,64,128]{2,1,0:T(8,128)S(1)}, f32[15,64,128]{2,1,0:T(8,128)S(1)}, u32[]{:S(2)}, u32[]{:S(2)}) collective-permute-start(f32[15,64,128]{2,1,0:T(8,128)S(1)} %get-tuple-element.78), channel_id=1, source_target_pairs={{0,2},{1,127},{2,4},{3,1},{4,6},{5,3},{6,8},{7,5},{8,10},{9,7},{10... | collective-permute-start | bytes 1474568 | tf_op jit(solution)/shard_map/ppermute | solution.py:366
  90.8 14.1 %collective-permute-start.17 = (f32[15,64,128]{2,1,0:T(8,128)S(1)}, f32[15,64,128]{2,1,0:T(8,128)S(1)}, u32[]{:S(2)}, u32[]{:S(2)}) collective-permute-start(f32[15,64,128]{2,1,0:T(8,128)S(1)} %get-tuple-element.79), channel_id=1, source_target_pairs={{1,3},{0,126},{3,5},{2,0},{5,7},{4,2},{7,9},{6,4},{9,11},{8,6},{11... | collective-permute-start | bytes 1474568 | tf_op jit(solution)/shard_map/ppermute | solution.py:366
  105.7 13.2 %collective-permute-start.19 = (f32[15,64,128]{2,1,0:T(8,128)S(1)}, f32[15,64,128]{2,1,0:T(8,128)S(1)}, u32[]{:S(2)}, u32[]{:S(2)}) collective-permute-start(f32[15,64,128]{2,1,0:T(8,128)S(1)} %get-tuple-element.82), channel_id=1, source_target_pairs={{1,3},{0,126},{3,5},{2,0},{5,7},{4,2},{7,9},{6,4},{9,11},{8,6},{11... | collective-permute-start | bytes 1474568 | tf_op jit(solution)/shard_map/ppermute | solution.py:366
  105.8 16.5 %collective-permute-start.18 = (f32[15,64,128]{2,1,0:T(8,128)S(1)}, f32[15,64,128]{2,1,0:T(8,128)S(1)}, u32[]{:S(2)}, u32[]{:S(2)}) collective-permute-start(f32[15,64,128]{2,1,0:T(8,128)S(1)} %get-tuple-element.81), channel_id=1, source_target_pairs={{0,2},{1,127},{2,4},{3,1},{4,6},{5,3},{6,8},{7,5},{8,10},{9,7},{10... | collective-permute-start | bytes 1474568 | tf_op jit(solution)/shard_map/ppermute | solution.py:366
  112.7 15.3 %collective-permute-start.21 = (f32[16,64,128]{2,1,0:T(8,128)S(1)}, f32[16,64,128]{2,1,0:T(8,128)S(1)}, u32[]{:S(2)}, u32[]{:S(2)}) collective-permute-start(f32[16,64,128]{2,1,0:T(8,128)S(1)} %get-tuple-element.80.own.current), channel_id=1, source_target_pairs={{0,1},{1,0},{2,3},{3,2},{4,5},{5,4},{6,7},{7,6},{8,9},{9,8},{10,11... | collective-permute-start | bytes 1572872 | tf_op jit(solution)/shard_map/ppermute | solution.py:370
  118.9 9.1 %collective-permute-start.20 = (f32[15,64,128]{2,1,0:T(8,128)S(1)}, f32[15,64,128]{2,1,0:T(8,128)S(1)}, u32[]{:S(2)}, u32[]{:S(2)}) collective-permute-start(f32[15,64,128]{2,1,0:T(8,128)S(1)} %collective-permute-done.19.second), channel_id=1, source_target_pairs={{0,1},{1,0},{2,3},{3,2},{4,5},{5,4},{6,7},{7,6},{8,9},{9,8},{10,11... | collective-permute-start | bytes 1474568 | tf_op jit(solution)/shard_map/ppermute | solution.py:370
  122.3 5.7 %collective-permute-start.22 = (f32[15,64,128]{2,1,0:T(8,128)S(1)}, f32[15,64,128]{2,1,0:T(8,128)S(1)}, u32[]{:S(2)}, u32[]{:S(2)}) collective-permute-start(f32[15,64,128]{2,1,0:T(8,128)S(1)} %collective-permute-done.18.first), channel_id=1, source_target_pairs={{0,1},{1,0},{2,3},{3,2},{4,5},{5,4},{6,7},{7,6},{8,9},{9,8},{10,11... | collective-permute-start | bytes 1474568 | tf_op jit(solution)/shard_map/ppermute | solution.py:370
  133.7 12.9 %collective-permute-start.23 = (f32[15,64,128]{2,1,0:T(8,128)S(1)}, f32[15,64,128]{2,1,0:T(8,128)S(1)}, u32[]{:S(2)}, u32[]{:S(2)}) collective-permute-start(f32[15,64,128]{2,1,0:T(8,128)S(1)} %get-tuple-element.86), channel_id=1, source_target_pairs={{0,2},{1,127},{2,4},{3,1},{4,6},{5,3},{6,8},{7,5},{8,10},{9,7},{10... | collective-permute-start | bytes 1474568 | tf_op jit(solution)/shard_map/ppermute | solution.py:366
  138.1 14.5 %collective-permute-start.24 = (f32[15,64,128]{2,1,0:T(8,128)S(1)}, f32[15,64,128]{2,1,0:T(8,128)S(1)}, u32[]{:S(2)}, u32[]{:S(2)}) collective-permute-start(f32[15,64,128]{2,1,0:T(8,128)S(1)} %get-tuple-element.87), channel_id=1, source_target_pairs={{1,3},{0,126},{3,5},{2,0},{5,7},{4,2},{7,9},{6,4},{9,11},{8,6},{11... | collective-permute-start | bytes 1474568 | tf_op jit(solution)/shard_map/ppermute | solution.py:366
  153.5 13.2 %collective-permute-start.26 = (f32[15,64,128]{2,1,0:T(8,128)S(1)}, f32[15,64,128]{2,1,0:T(8,128)S(1)}, u32[]{:S(2)}, u32[]{:S(2)}) collective-permute-start(f32[15,64,128]{2,1,0:T(8,128)S(1)} %get-tuple-element.90), channel_id=1, source_target_pairs={{1,3},{0,126},{3,5},{2,0},{5,7},{4,2},{7,9},{6,4},{9,11},{8,6},{11... | collective-permute-start | bytes 1474568 | tf_op jit(solution)/shard_map/ppermute | solution.py:366
  153.6 16.0 %collective-permute-start.25 = (f32[15,64,128]{2,1,0:T(8,128)S(1)}, f32[15,64,128]{2,1,0:T(8,128)S(1)}, u32[]{:S(2)}, u32[]{:S(2)}) collective-permute-start(f32[15,64,128]{2,1,0:T(8,128)S(1)} %get-tuple-element.89), channel_id=1, source_target_pairs={{0,2},{1,127},{2,4},{3,1},{4,6},{5,3},{6,8},{7,5},{8,10},{9,7},{10... | collective-permute-start | bytes 1474568 | tf_op jit(solution)/shard_map/ppermute | solution.py:366
  160.4 14.9 %collective-permute-start.28 = (f32[16,64,128]{2,1,0:T(8,128)S(1)}, f32[16,64,128]{2,1,0:T(8,128)S(1)}, u32[]{:S(2)}, u32[]{:S(2)}) collective-permute-start(f32[16,64,128]{2,1,0:T(8,128)S(1)} %get-tuple-element.88.own.current), channel_id=1, source_target_pairs={{0,1},{1,0},{2,3},{3,2},{4,5},{5,4},{6,7},{7,6},{8,9},{9,8},{10,11... | collective-permute-start | bytes 1572872 | tf_op jit(solution)/shard_map/ppermute | solution.py:370
  166.6 8.7 %collective-permute-start.27 = (f32[15,64,128]{2,1,0:T(8,128)S(1)}, f32[15,64,128]{2,1,0:T(8,128)S(1)}, u32[]{:S(2)}, u32[]{:S(2)}) collective-permute-start(f32[15,64,128]{2,1,0:T(8,128)S(1)} %collective-permute-done.26.second), channel_id=1, source_target_pairs={{0,1},{1,0},{2,3},{3,2},{4,5},{5,4},{6,7},{7,6},{8,9},{9,8},{10,11... | collective-permute-start | bytes 1474568 | tf_op jit(solution)/shard_map/ppermute | solution.py:370
  169.6 5.8 %collective-permute-start.29 = (f32[15,64,128]{2,1,0:T(8,128)S(1)}, f32[15,64,128]{2,1,0:T(8,128)S(1)}, u32[]{:S(2)}, u32[]{:S(2)}) collective-permute-start(f32[15,64,128]{2,1,0:T(8,128)S(1)} %collective-permute-done.25.first), channel_id=1, source_target_pairs={{0,1},{1,0},{2,3},{3,2},{4,5},{5,4},{6,7},{7,6},{8,9},{9,8},{10,11... | collective-permute-start | bytes 1474568 | tf_op jit(solution)/shard_map/ppermute | solution.py:370
  181.0 12.9 %collective-permute-start.30 = (f32[15,64,128]{2,1,0:T(8,128)S(1)}, f32[15,64,128]{2,1,0:T(8,128)S(1)}, u32[]{:S(2)}, u32[]{:S(2)}) collective-permute-start(f32[15,64,128]{2,1,0:T(8,128)S(1)} %get-tuple-element.94), channel_id=1, source_target_pairs={{0,2},{1,127},{2,4},{3,1},{4,6},{5,3},{6,8},{7,5},{8,10},{9,7},{10... | collective-permute-start | bytes 1474568 | tf_op jit(solution)/shard_map/ppermute | solution.py:366
  185.4 14.5 %collective-permute-start.31 = (f32[15,64,128]{2,1,0:T(8,128)S(1)}, f32[15,64,128]{2,1,0:T(8,128)S(1)}, u32[]{:S(2)}, u32[]{:S(2)}) collective-permute-start(f32[15,64,128]{2,1,0:T(8,128)S(1)} %get-tuple-element.95), channel_id=1, source_target_pairs={{1,3},{0,126},{3,5},{2,0},{5,7},{4,2},{7,9},{6,4},{9,11},{8,6},{11... | collective-permute-start | bytes 1474568 | tf_op jit(solution)/shard_map/ppermute | solution.py:366
  201.7 1.9 collective-permute-start.32
  (2 other events, 4.6 us)
